TPU v7x, 512 devices: a whole 4x4x16 slice. The times are simulated.
512 devices in a mesh: batch: 32 (over z, core), feat: 16 (over y, x).
Axes of the slice: x: 4, y: 4, z: 16, core: 2. Of those that a mesh axis runs over, the one named last changes fastest.
Arguments:
- view_one: bfloat16 [512, 16384], P('batch', 'feat'), may hold values from -700 to 700, as said below
- view_two: bfloat16 [512, 16384], P('batch', 'feat'), may hold values from -700 to 700
Outputs:
- row_loss: float32 [16384], P('feat')
- grad_one: float32 [512, 16384], P('batch', 'feat')
- grad_two: float32 [512, 16384], P('batch', 'feat')
Inputs may be any that keep to these rules, and one draw needn't show every extreme that they name: Both views of a row come from one image: every column of view_two is correlated with the same column of view_one.
All inputs are finite; a program needn't handle non-finite values.
Results may differ from a plain program's by a relative error of at most 0.01.
Values may be sent and summed in bfloat16 or wider, within the bound.
No kernel may reach another device: no remote copies, remote signals or barrier semaphores. Data moves between devices by JAX's collectives and lax.ppermute only.
A program may use at most 64 MiB of HBM per device.

v0:
```python
import jax
import jax.numpy as jnp
from jax import lax
from jax.sharding import PartitionSpec as P

EPSILON = 1e-05
LAMBDA = 0.0051


def local(view_one, view_two):
    own_rows = view_one.shape[0]
    own_width = view_one.shape[1]
    batch_ways = lax.axis_size("batch")
    column_ways = lax.axis_size("feat")
    all_rows = own_rows * batch_ways
    piece_width = own_width // batch_ways
    set_width = piece_width * column_ways
    values_one = view_one.astype(jnp.float32)
    values_two = view_two.astype(jnp.float32)
    sums_one, sums_two = lax.psum(
        (jnp.sum(values_one, axis=0), jnp.sum(values_two, axis=0)), "batch"
    )
    shifted_one = values_one - sums_one / all_rows
    shifted_two = values_two - sums_two / all_rows
    spread_one, spread_two = lax.psum(
        (jnp.sum(shifted_one * shifted_one, axis=0), jnp.sum(shifted_two * shifted_two, axis=0)),
        "batch",
    )
    scaling_one = lax.rsqrt(spread_one / all_rows + EPSILON)
    scaling_two = lax.rsqrt(spread_two / all_rows + EPSILON)
    normed_one = (shifted_one * scaling_one).astype(jnp.bfloat16)
    normed_two = (shifted_two * scaling_two).astype(jnp.bfloat16)
    float_one = normed_one.astype(jnp.float32)
    float_two = normed_two.astype(jnp.float32)
    batch_place = lax.axis_index("batch")
    feat_place = lax.axis_index("feat")
    tall_one = lax.all_gather(normed_one, "batch", axis=0, tiled=True)
    parted = lax.all_to_all(normed_two, "batch", split_axis=1, concat_axis=0, tiled=True)
    tall_two = lax.all_gather(parted, "feat", axis=1, tiled=True)
    correlation = (
        lax.dot_general(
            tall_one, tall_two, (((0,), (0,)), ((), ())), preferred_element_type=jnp.float32
        )
        / all_rows
    )
    set_index = jnp.arange(set_width, dtype=jnp.int32)
    global_cols = (
        set_index // piece_width * own_width + batch_place * piece_width + set_index % piece_width
    )
    global_rows = feat_place * own_width + jnp.arange(own_width, dtype=jnp.int32)
    diag_mask = global_rows[:, None] == global_cols[None, :]
    on_diag = jnp.sum(jnp.where(diag_mask, correlation, 0.0), axis=1)
    has_diag = jnp.any(diag_mask, axis=1)
    off_squares = jnp.sum(jnp.where(diag_mask, 0.0, correlation * correlation), axis=1)
    local_terms = jnp.where(has_diag, (1.0 - on_diag) * (1.0 - on_diag), 0.0) + LAMBDA * off_squares
    row_loss = lax.psum(local_terms, "batch")
    slopes = jnp.where(diag_mask, -2.0 * (1.0 - correlation), 2.0 * LAMBDA * correlation)
    tall_two_float = tall_two.astype(jnp.float32)
    first_up = lax.psum_scatter(
        lax.dot_general(
            tall_two_float,
            slopes,
            (((1,), (1,)), ((), ())),
            precision=lax.Precision.HIGHEST,
            preferred_element_type=jnp.float32,
        ),
        "batch",
        scatter_dimension=0,
        tiled=True,
    )
    second_part = jnp.dot(tall_one.astype(jnp.float32), slopes, precision=lax.Precision.HIGHEST)
    summed = lax.psum_scatter(second_part, "feat", scatter_dimension=1, tiled=True)
    second_up = lax.all_to_all(summed, "batch", split_axis=0, concat_axis=1, tiled=True)
    first_sum, first_dot, second_sum, second_dot = lax.psum(
        (
            jnp.sum(first_up, axis=0),
            jnp.sum(first_up * float_one, axis=0),
            jnp.sum(second_up, axis=0),
            jnp.sum(second_up * float_two, axis=0),
        ),
        "batch",
    )
    grad_one = scaling_one * (first_up - first_sum / all_rows - float_one * (first_dot / all_rows))
    grad_two = scaling_two * (
        second_up - second_sum / all_rows - float_two * (second_dot / all_rows)
    )
    return (row_loss, grad_one, grad_two)


def solution(mesh):
    in_specs = (P("batch", "feat"), P("batch", "feat"))
    out_specs = (P("feat"), P("batch", "feat"), P("batch", "feat"))
    return jax.shard_map(local, mesh=mesh, in_specs=in_specs, out_specs=out_specs, check_vma=False)
```

profile of v0, /device:TPU:1, one launch (start us, length us, event | category | flops | bytes accessed | tf_op | source)
XLA Modules:
  0.0 481.6 jit_solution(7885543577302147695)
XLA Ops:
  7.2 0.8 convert_reduce_fusion.1
  8.0 0.8 convert_reduce_fusion
  8.8 54.3 %all-reduce.2 = (f32[1024]{0:T(1024)S(1)}, f32[1024]{0:T(1024)S(1)}) all-reduce(f32[1024]{0:T(1024)S(1)} %convert_reduce_fusion, f32[1024]{0:T(1024)S(1)} %convert_reduce_fusion.1), channel_id=1, replica_groups=mesh['batch'=32,'feat'=16] {'batch'}, use_global_device_ids=true, to_apply=%region_6.0 | all-reduce | flops 2048 | bytes 16384 | tf_op jit(solution)/shard_map/psum | solution.py:20
  63.1 0.8 fusion.20
  63.9 0.8 fusion.22
  64.6 49.1 %all-reduce.1 = (f32[1024]{0:T(1024)S(1)}, f32[1024]{0:T(1024)S(1)}) all-reduce(f32[1024]{0:T(1024)S(1)} %fusion.20, f32[1024]{0:T(1024)S(1)} %fusion.22), channel_id=1, replica_groups=mesh['batch'=32,'feat'=16] {'batch'}, use_global_device_ids=true, to_apply=%region_8.9 | all-reduce | flops 2048 | bytes 16384 | tf_op jit(solution)/shard_map/psum | solution.py:25
  113.8 1.4 fusion.23
  115.2 0.8 fusion.21
  116.0 0.1 all_to_all.28
  116.2 0.8 reshape.48
  116.9 7.0 %all-to-all-start = ((bf16[32,2,256]{2,1,0:T(2,128)(2,1)}), bf16[32,2,256]{2,1,0:T(2,128)(2,1)S(1)}, u32[]{:S(2)}, u32[]{:S(2)}) async-start(bf16[32,2,256]{2,1,0:T(2,128)(2,1)} %reshape.48), calls=%async_computation | async-start | bytes 65536 | tf_op jit(solution)/shard_map/all_to_all | solution.py:38
  124.0 12.0 %all-to-all-done = bf16[32,2,256]{2,1,0:T(2,128)(2,1)S(1)} async-done(((bf16[32,2,256]{2,1,0:T(2,128)(2,1)}), bf16[32,2,256]{2,1,0:T(2,128)(2,1)S(1)}, u32[]{:S(2)}, u32[]{:S(2)}) %all-to-all-start) | async-done | bytes 32800 | tf_op jit(solution)/shard_map/all_to_all | solution.py:38
  136.1 0.1 reshape.49
  136.3 20.1 %all_gather.7 = bf16[512,512]{0,1:T(8,128)(2,1)S(1)} all-gather(bf16[512,32]{0,1:T(8,128)(2,1)S(1)} %copy.12), channel_id=1, replica_groups=mesh['batch'=32,'feat'=16] {'feat'}, dimensions={1}, use_global_device_ids=true | all-gather | bytes 557056 | tf_op jit(solution)/shard_map/all_gather | solution.py:39
  156.4 25.6 %all-gather.2.cloned.1.call-done = bf16[512,1024]{1,0:T(8,128)(2,1)} async-done(((bf16[16,1024]{1,0:T(8,128)(2,1)}), bf16[512,1024]{1,0:T(8,128)(2,1)}) %all-gather.2.cloned.1.call-update) | async-done | bytes 1048592 | tf_op jit(solution)/shard_map/all_gather | solution.py:37
  182.0 2.2 fusion
  184.2 3.1 fusion.2
  187.4 3.8 fusion.3
  191.2 79.7 %reduce-scatter.5.cloned.1.call-done = f32[512,32]{0,1:T(8,128)} async-done(((f32[512,512]{0,1:T(8,128)}), f32[512,32]{0,1:T(8,128)}) %reduce-scatter.5.cloned.1.call-update) | async-done | bytes 65552 | tf_op jit(solution)/shard_map/reduce_scatter | solution.py:72
  270.8 1.0 copy.13
  271.8 0.8 reshape.50
  272.6 14.6 %all-to-all-start.1 = ((f32[32,1,512]{2,1,0:T(1,128)}), f32[32,1,512]{2,1,0:T(1,128)S(1)}, u32[]{:S(2)}, u32[]{:S(2)}) async-start(f32[32,1,512]{2,1,0:T(1,128)} %reshape.50), calls=%async_computation.3 | async-start | bytes 131072 | tf_op jit(solution)/shard_map/all_to_all | solution.py:73
  287.2 0.4 compare_reduce_fusion
  287.6 12.7 %all-to-all-done.1 = f32[32,1,512]{2,1,0:T(1,128)S(1)} async-done(((f32[32,1,512]{2,1,0:T(1,128)}), f32[32,1,512]{2,1,0:T(1,128)S(1)}, u32[]{:S(2)}, u32[]{:S(2)}) %all-to-all-start.1) | async-done | bytes 65568 | tf_op jit(solution)/shard_map/all_to_all | solution.py:73
  300.3 0.5 broadcast.103
  300.8 0.8 reduce.1
  301.9 0.1 all_to_all.35
  302.1 79.8 %reduce-scatter.3.cloned.1.call-done = f32[16,1024]{1,0:T(8,128)} async-done(((f32[512,1024]{1,0:T(8,128)}), f32[16,1024]{1,0:T(8,128)}) %reduce-scatter.3.cloned.1.call-update) | async-done | bytes 65552 | tf_op jit(solution)/shard_map/reduce_scatter | solution.py:59
  381.9 0.9 fusion.48
  382.8 90.2 %all-reduce = (f32[1024]{0:T(1024)}, f32[1024]{0:T(1024)S(1)}, f32[1024]{0:T(1024)S(1)}, f32[1024]{0:T(1024)S(1)}, f32[1024]{0:T(1024)S(1)}) all-reduce(f32[1024]{0:T(1024)S(1)} %multiply_add_fusion, f32[1024]{0:T(1024)S(1)} %get-tuple-element.6, f32[1024]{0:T(1024)S(1)} %get-tuple-element.5, ...), channel_id=1, replica_groups=mesh['batch'=32,'feat'=16] {'batch'}, use_global_device_ids=true, to_apply=%region_11.12 | all-reduce | flops 5120 | bytes 40960 | tf_op jit(solution)/shard_map/psum | solution.py:56
  472.9 0.7 fusion.29
  473.6 1.5 fusion.26
  (29 shorter events, 0.7 us)
Async XLA Ops:
  7.2 174.8 %all-gather.2.cloned.1.call-start = ((), (), s32[]{:S(2)}) async-start(), calls=%async_computation.4 | async-start | bytes 1081344 | tf_op jit(solution)/shard_map/all_gather | solution.py:37
  116.9 19.2 %all-to-all-start = ((bf16[32,2,256]{2,1,0:T(2,128)(2,1)}), bf16[32,2,256]{2,1,0:T(2,128)(2,1)S(1)}, u32[]{:S(2)}, u32[]{:S(2)}) async-start(bf16[32,2,256]{2,1,0:T(2,128)(2,1)} %reshape.48), calls=%async_computation | async-start | bytes 65536 | tf_op jit(solution)/shard_map/all_to_all | solution.py:38
  124.0 146.9 %reduce-scatter.5.cloned.1.call-start = ((), (), s32[]{:S(2)}) async-start(), calls=%async_computation.6 | async-start | bytes 1114112 | tf_op jit(solution)/shard_map/reduce_scatter | solution.py:72
  182.0 2.3 copy-start.2
  187.3 194.6 %reduce-scatter.3.cloned.1.call-start = ((), (), s32[]{:S(2)}) async-start(), calls=%async_computation.5 | async-start | bytes 2162688 | tf_op jit(solution)/shard_map/reduce_scatter | solution.py:59
  191.1 110.9 %copy-start = (bf16[16,1024]{1,0:T(8,128)(2,1)S(1)}, bf16[16,1024]{1,0:T(8,128)(2,1)}, u32[]{:S(2)}) copy-start(bf16[16,1024]{1,0:T(8,128)(2,1)} %param.3) | copy-start | bytes 98308
  191.1 190.7 %copy-start.1 = (bf16[16,1024]{1,0:T(8,128)(2,1)S(1)}, bf16[16,1024]{1,0:T(8,128)(2,1)}, u32[]{:S(2)}) copy-start(bf16[16,1024]{1,0:T(8,128)(2,1)} %param.2) | copy-start | bytes 98308
  272.6 27.7 %all-to-all-start.1 = ((f32[32,1,512]{2,1,0:T(1,128)}), f32[32,1,512]{2,1,0:T(1,128)S(1)}, u32[]{:S(2)}, u32[]{:S(2)}) async-start(f32[32,1,512]{2,1,0:T(1,128)} %reshape.50), calls=%async_computation.3 | async-start | bytes 131072 | tf_op jit(solution)/shard_map/all_to_all | solution.py:73
Sparse Core Ops, SparseCore 0:
  115.3 66.6 all-gather.1
  187.4 83.3 reduce-scatter.4
  273.9 107.9 reduce-scatter.2
where the time goes:
time: 485 us; the launch traced here: 482 us
  blocking collectives  214 us (44%)
  waiting for transfers between devices  210 us (43%)
  starting transfers between devices  21.7 us (4%)
  between operations  14 us (3%)
  other arithmetic  9.55 us (2%)
  matrix products  9.07 us (2%)
    psum x1, blocking collectives, local(): row_loss = lax.psum(local_terms, 'batch')  90.2 us
    reduce_scatter x1, waiting for transfers between devices, local(): lax.psum_scatter(lax.dot_general(tall_two_float, slopes, (((1,), (1,)), (...  79.8 us
    reduce_scatter x1, waiting for transfers between devices, local(): lax.psum_scatter(second_part, 'feat', scatter_dimension=1, tiled=True)  79.7 us
    psum x1, blocking collectives, local(): lax.psum((jnp.sum(values_one, axis=0), jnp.sum(values_two, axis=0)), 'bat...  54.3 us
    psum x1, blocking collectives, local(): lax.psum((jnp.sum(shifted_one * shifted_one, axis=0), jnp.sum(shifted_two...  49.1 us
    all_gather x1, waiting for transfers between devices, local(): tall_one = lax.all_gather(normed_one, 'batch', axis=0, tiled=True)  25.6 us
    all_gather x1, blocking collectives, local(): tall_two = lax.all_gather(parted, 'feat', axis=1, tiled=True)  20.1 us
    all_to_all x1, starting transfers between devices, local(): lax.all_to_all(summed, 'batch', split_axis=0, concat_axis=1, tiled=True)  14.6 us
  transfers between devices with their start and end apart: 5, of which 5 were waited for; matrix products, arithmetic and copies ran while one was open for 2% of the time, Pallas kernels for 0%

commit v1 on v0

v1 whole, which is shorter than its diff:
```python
import jax
import jax.numpy as jnp
from jax import lax
from jax.sharding import Mesh, PartitionSpec as P

EPSILON = 1e-05
LAMBDA = 0.0051
FEATURES = 16384
BATCH = 512

CUTS = (4, 4, 2, 4, 4)
NAMES = ("zh", "zl", "c", "y", "x")
CHIPS = ("zh", "zl")
FEAT = ("y", "x")
SLICES = 4


def swap(values, axes):
    return lax.all_to_all(values, axes, split_axis=0, concat_axis=0)


def local(view_one, view_two):
    rows, width = view_one.shape
    part = width // SLICES
    core = lax.axis_index("c")
    group = lax.axis_index("zh")

    both = jnp.stack([view_one, view_two]).reshape(2, rows, SLICES, part)
    both = jnp.transpose(both, (2, 0, 1, 3))
    sent = jnp.broadcast_to(both[None], (4,) + both.shape).reshape(16, 2, rows, part)
    chips = swap(sent, CHIPS)
    whole = lax.all_gather(chips, "c")
    views = jnp.transpose(whole, (2, 0, 1, 3, 4)).reshape(2, BATCH, part)

    values = views.astype(jnp.float32)
    center = jnp.sum(values, axis=1, keepdims=True) / BATCH
    shifted = values - center
    spread = jnp.sum(shifted * shifted, axis=1, keepdims=True) / BATCH
    scaling = lax.rsqrt(spread + EPSILON)
    normed = (shifted * scaling).astype(jnp.bfloat16)
    mine = lax.dynamic_index_in_dim(normed, core, 0, keepdims=False)
    other = lax.dynamic_index_in_dim(normed, 1 - core, 0, keepdims=False)
    scale_mine = lax.dynamic_index_in_dim(scaling, core, 0, keepdims=False)

    eye = jnp.eye(BATCH, dtype=jnp.float32)
    gram = lax.dot_general(
        other, other, (((1,), (1,)), ((), ())), preferred_element_type=jnp.float32
    )
    gram = (gram - part * eye).astype(jnp.bfloat16).reshape(16, BATCH // 16, BATCH)
    strip = jnp.sum(swap(gram, FEAT).astype(jnp.float32), axis=0).astype(jnp.bfloat16)
    strip = swap(jnp.broadcast_to(strip[None], (SLICES,) + strip.shape), "zl")
    strip = jnp.sum(strip.astype(jnp.float32), axis=0).astype(jnp.bfloat16)
    total = swap(jnp.broadcast_to(strip[None], (16,) + strip.shape), FEAT).reshape(BATCH, BATCH)

    float_mine = mine.astype(jnp.float32)
    float_other = other.astype(jnp.float32)
    on_diag = jnp.sum(float_mine * float_other, axis=0, keepdims=True) / BATCH
    slope = -2.0 * (1.0 - on_diag) - 2.0 * LAMBDA * on_diag
    product = jnp.dot(total, mine, preferred_element_type=jnp.float32) + FEATURES * float_mine
    squares = jnp.sum(product * float_mine, axis=0, keepdims=True) / (BATCH * BATCH)
    loss = (1.0 - on_diag) * (1.0 - on_diag) + LAMBDA * (squares - on_diag * on_diag)
    up = (2.0 * LAMBDA / BATCH) * product + slope * float_other
    first = jnp.sum(up, axis=0, keepdims=True) / BATCH
    second = jnp.sum(up * float_mine, axis=0, keepdims=True) / BATCH
    grad = scale_mine * (up - first - float_mine * second)

    grad = grad.reshape(2, 4, 4, rows, part)
    grad = lax.dynamic_index_in_dim(grad, group, 1, keepdims=False)
    grad = jnp.transpose(grad, (1, 0, 2, 3)).reshape(8, rows, part).astype(jnp.bfloat16)
    high = loss.astype(jnp.bfloat16)
    rest = loss - high.astype(jnp.float32)
    middle = rest.astype(jnp.bfloat16)
    low = (rest - middle.astype(jnp.float32)).astype(jnp.bfloat16)
    tail = jnp.concatenate([high, middle, low, jnp.zeros((13, part), jnp.bfloat16)], axis=0)
    tail = jnp.broadcast_to(tail[None], (8,) + tail.shape)
    out = swap(jnp.concatenate([grad, tail], axis=1), ("zl", "c")).astype(jnp.float32)
    out = out.reshape(SLICES, 2, rows + 16, part)
    row_loss = (out[:, 0, rows] + (out[:, 0, rows + 1] + out[:, 0, rows + 2])).reshape(width)
    grads = jnp.transpose(out[:, :, :rows], (1, 2, 0, 3)).reshape(2, rows, width)
    return (row_loss, grads[0], grads[1])


def solution(mesh):
    cut = Mesh(mesh.devices.reshape(CUTS), NAMES)
    spread = P(("zh", "zl", "c"), FEAT)
    return jax.shard_map(
        local, mesh=cut, in_specs=(spread, spread), out_specs=(P(FEAT), spread, spread), check_vma=False
    )
```

time: 485 us -> 95.4 us (0.20)
  waiting for transfers between devices: 210 us -> 21.9 us
  blocking collectives: 214 us -> 46.5 us
  between operations: 14 us -> 0.85 us
  matrix products: 9.07 us -> 0.71 us
  other arithmetic: 9.55 us -> 1.69 us
    psum x3 -> x0, blocking collectives: 194 us -> none  [the longest x1 90.2 us: local(): row_loss = lax.psum(local_terms, 'batch')]
    reduce_scatter x2 -> x0, waiting for transfers between devices: 159 us -> none  [the longest x1 79.8 us: local(): lax.psum_scatter(lax.dot_general(tall_two_float, slopes, (((1,), (1,)), (...]
    all_to_all x0 -> x3, blocking collectives: none -> 38.6 us  [swap(): return lax.all_to_all(values, axes, split_axis=0, concat_axis=0)]
    all_gather x1 -> x0, waiting for transfers between devices: 25.6 us -> none  [local(): tall_one = lax.all_gather(normed_one, 'batch', axis=0, tiled=True)]
    all_gather x1, blocking collectives: 20.1 us -> 7.98 us  [local(): whole = lax.all_gather(chips, 'c')]
    dot_general x3 -> x2, matrix products: 9.07 us -> 0.71 us  [the longest x1 0.38 us: local(): jnp.dot(total, mine, preferred_element_type=jnp.float32)]
  transfers between devices with their start and end apart: 5 -> 2, of which waited for: 5 -> 2; matrix products, arithmetic and copies ran while one was open for 2% -> 0% of each run, Pallas kernels for 0% -> 0%
where the time goes in v1:
time: 95.4 us; the launch traced here: 95 us
  blocking collectives  46.5 us (49%)
  waiting for transfers between devices  21.9 us (23%)
  starting transfers between devices  19.3 us (20%)
  local copies, waits for them, and re-layouts  3.99 us (4%)
  other arithmetic  1.69 us (2%)
    all_to_all x3, blocking collectives, swap(): return lax.all_to_all(values, axes, split_axis=0, concat_axis=0)  38.6 us
    all_to_all x2, waiting for transfers between devices, swap(): return lax.all_to_all(values, axes, split_axis=0, concat_axis=0)  21.9 us
    all_to_all x2, starting transfers between devices, swap(): return lax.all_to_all(values, axes, split_axis=0, concat_axis=0)  19.3 us
    all_gather x1, blocking collectives, local(): whole = lax.all_gather(chips, 'c')  7.98 us
  transfers between devices with their start and end apart: 2, of which 2 were waited for; matrix products, arithmetic and copies ran while one was open for 0% of the time, Pallas kernels for 0%

profile of v1, /device:TPU:1, one launch (start us, length us, event | category | flops | bytes accessed | tf_op | source)
XLA Modules:
  0.0 95.0 jit_solution(11489105008202369049)
XLA Ops:
  0.6 0.0 copy-start
  0.6 0.8 stack.10
  1.4 0.0 copy-done
  1.5 0.7 broadcast_in_dim.10
  2.3 15.7 %all-to-all-start = ((bf16[16,2,16,256]{3,2,1,0:T(8,128)(2,1)}), bf16[16,2,16,256]{3,2,1,0:T(8,128)(2,1)S(1)}, u32[]{:S(2)}, u32[]{:S(2)}) async-start(bf16[16,2,16,256]{3,2,1,0:T(8,128)(2,1)} %bitcast.1), calls=%async_computation | async-start | bytes 524288 | tf_op jit(solution)/shard_map/all_to_all | solution.py:19
  18.0 13.1 %all-to-all-done = bf16[16,2,16,256]{3,2,1,0:T(8,128)(2,1)S(1)} async-done(((bf16[16,2,16,256]{3,2,1,0:T(8,128)(2,1)}), bf16[16,2,16,256]{3,2,1,0:T(8,128)(2,1)S(1)}, u32[]{:S(2)}, u32[]{:S(2)}) %all-to-all-start) | async-done | bytes 262176 | tf_op jit(solution)/shard_map/all_to_all | solution.py:19
  31.1 8.0 %all-gather = bf16[32,2,16,256]{3,2,1,0:T(8,128)(2,1)S(1)} all-gather(bf16[16,2,16,256]{3,2,1,0:T(8,128)(2,1)S(1)} %all-to-all-done), channel_id=2, replica_groups=mesh['zh'=4,'zl'=4,'c'=2,'y'=4,'x'=4] {'c'}, dimensions={0}, use_global_device_ids=true | all-gather | bytes 786432 | tf_op jit(solution)/shard_map/all_gather | solution.py:32
  39.1 0.1 convert_bitcast_fusion
  39.2 0.1 fusion.9
  39.4 0.2 multiply_reduce_fusion
  39.5 0.1 copy.23
  39.6 0.1 fusion.2
  39.8 0.3 fusion
  40.1 17.3 %all_to_all.25 = bf16[16,32,512]{2,1,0:T(8,128)(2,1)S(1)} all-to-all(bf16[16,32,512]{2,1,0:T(8,128)(2,1)S(1)} %bitcast.64), channel_id=1, replica_groups=mesh['zh'=4,'zl'=4,'c'=2,'y'=4,'x'=4] {'y','x'}, dimensions={0} | all-to-all | bytes 1048576 | tf_op jit(solution)/shard_map/all_to_all | solution.py:19
  57.4 0.1 reduce_sum.80
  57.5 8.6 %all_to_all.26 = bf16[4,32,512]{2,1,0:T(8,128)(2,1)S(1)} all-to-all(bf16[4,32,512]{2,1,0:T(8,128)(2,1)S(1)} %broadcast_in_dim.11), channel_id=1, replica_groups=mesh['zh'=4,'zl'=4,'c'=2,'y'=4,'x'=4] {'zl'}, dimensions={0} | all-to-all | bytes 262144 | tf_op jit(solution)/shard_map/all_to_all | solution.py:19
  66.1 0.8 broadcast_in_dim.12
  67.0 3.6 %all-to-all-start.3 = ((bf16[16,32,512]{2,1,0:T(8,128)(2,1)}), bf16[16,32,512]{2,1,0:T(8,128)(2,1)S(1)}, u32[]{:S(2)}, u32[]{:S(2)}) async-start(bf16[16,32,512]{2,1,0:T(8,128)(2,1)} %broadcast_in_dim.12), calls=%async_computation.3 | async-start | bytes 1048576 | tf_op jit(solution)/shard_map/all_to_all | solution.py:19
  70.6 0.1 pad.5.clone
  70.7 0.1 fusion.4
  70.8 8.7 %all-to-all-done.3 = bf16[16,32,512]{2,1,0:T(8,128)(2,1)S(1)} async-done(((bf16[16,32,512]{2,1,0:T(8,128)(2,1)}), bf16[16,32,512]{2,1,0:T(8,128)(2,1)S(1)}, u32[]{:S(2)}, u32[]{:S(2)}) %all-to-all-start.3) | async-done | bytes 524320 | tf_op jit(solution)/shard_map/all_to_all | solution.py:19
  79.5 0.4 fusion.14
  79.9 0.2 fusion.7
  80.2 0.1 maximum_maximum_fusion
  80.3 12.6 %all_to_all.27 = bf16[8,32,256]{2,1,0:T(8,128)(2,1)S(1)} all-to-all(bf16[8,32,256]{2,1,0:T(8,128)(2,1)S(1)} %pad_maximum_fusion), channel_id=1, replica_groups=mesh['zh'=4,'zl'=4,'c'=2,'y'=4,'x'=4] {'zl','c'}, dimensions={0} | all-to-all | bytes 262144 | tf_op jit(solution)/shard_map/all_to_all | solution.py:19
  92.9 0.6 fusion.15
  93.6 0.6 copy.28
  94.3 0.6 copy.29
  (23 shorter events, 0.3 us)
Async XLA Ops:
  0.6 0.8 copy-start
  2.3 28.9 %all-to-all-start = ((bf16[16,2,16,256]{3,2,1,0:T(8,128)(2,1)}), bf16[16,2,16,256]{3,2,1,0:T(8,128)(2,1)S(1)}, u32[]{:S(2)}, u32[]{:S(2)}) async-start(bf16[16,2,16,256]{3,2,1,0:T(8,128)(2,1)} %bitcast.1), calls=%async_computation | async-start | bytes 524288 | tf_op jit(solution)/shard_map/all_to_all | solution.py:19
  67.0 12.5 %all-to-all-start.3 = ((bf16[16,32,512]{2,1,0:T(8,128)(2,1)}), bf16[16,32,512]{2,1,0:T(8,128)(2,1)S(1)}, u32[]{:S(2)}, u32[]{:S(2)}) async-start(bf16[16,32,512]{2,1,0:T(8,128)(2,1)} %broadcast_in_dim.12), calls=%async_computation.3 | async-start | bytes 1048576 | tf_op jit(solution)/shard_map/all_to_all | solution.py:19

commit v2 on v1

v2 whole, which is shorter than its diff:
```python
import jax
import jax.numpy as jnp
from jax import lax
from jax.experimental import pallas as pl
from jax.experimental.pallas import tpu as pltpu
from jax.sharding import Mesh, PartitionSpec as P

EPSILON = 1e-05
LAMBDA = 0.0051
FEATURES = 16384
BATCH = 512

CUTS = (4, 4, 2, 4, 4)
NAMES = ("zh", "zl", "c", "y", "x")
CHIPS = ("zh", "zl")
FEAT = ("y", "x")
GROUPS = 4
SLICES = 4
OWNERS = 16
ROWS = 16
WIDTH = 1024
PART = WIDTH // SLICES
SIDE = 128
BLOCKS = BATCH // SIDE
PACKED = BLOCKS * (BLOCKS + 1) // 2 * SIDE
CHUNK = PACKED // OWNERS
NT = (((1,), (1,)), ((), ()))
TN = (((0,), (0,)), ((), ()))


def swap(values, axes):
    return lax.all_to_all(values, axes, split_axis=0, concat_axis=0)


def place(i, j):
    return (i * (i + 1) // 2 + j) * SIDE


def call(kernel, out_shape, flops, *operands, scratch=(), scalars=0):
    moved = sum(o.size * o.dtype.itemsize for o in operands)
    specs = [pl.BlockSpec(memory_space=pltpu.SMEM)] * scalars
    specs += [pl.BlockSpec(memory_space=pltpu.VMEM)] * (len(operands) - scalars)
    many = isinstance(out_shape, (list, tuple))
    whole = pl.BlockSpec(memory_space=pltpu.VMEM)
    return pl.pallas_call(
        kernel,
        out_shape=out_shape,
        in_specs=specs,
        out_specs=[whole] * len(out_shape) if many else whole,
        scratch_shapes=list(scratch),
        cost_estimate=pl.CostEstimate(flops=flops, bytes_accessed=moved, transcendentals=0),
        compiler_params=pltpu.CompilerParams(vmem_limit_bytes=16 * 1024 * 1024),
    )(*operands)


def spread_kernel(one_ref, two_ref, out_ref):
    for k in range(SLICES):
        columns = slice(k * PART, (k + 1) * PART)
        one, two = one_ref[:, columns], two_ref[:, columns]
        for h in range(GROUPS):
            out_ref[h * SLICES + k, 0] = one
            out_ref[h * SLICES + k, 1] = two


def gram_kernel(core_ref, whole_ref, normed_ref, scaling_ref, packed_ref):
    for v in range(2):
        values = whole_ref[:, v].astype(jnp.float32).reshape(BATCH, PART)
        center = jnp.sum(values, axis=0, keepdims=True) / BATCH
        shifted = values - center
        spread = jnp.sum(shifted * shifted, axis=0, keepdims=True) / BATCH
        scaling = lax.rsqrt(spread + EPSILON)
        scaling_ref[v] = scaling
        normed_ref[v] = (shifted * scaling).astype(jnp.bfloat16)
    other = 1 - core_ref[0]
    row = lax.broadcasted_iota(jnp.int32, (SIDE, SIDE), 0)
    column = lax.broadcasted_iota(jnp.int32, (SIDE, SIDE), 1)
    mean_diag = jnp.where(row == column, float(PART), 0.0)
    for i in range(BLOCKS):
        left = normed_ref[other, i * SIDE : (i + 1) * SIDE]
        for j in range(i + 1):
            right = normed_ref[other, j * SIDE : (j + 1) * SIDE]
            block = lax.dot_general(left, right, NT, preferred_element_type=jnp.float32)
            if i == j:
                block = block - mean_diag
            packed_ref[place(i, j) : place(i, j) + SIDE] = block.astype(jnp.bfloat16)


def sum_kernel(parts_ref, out_ref):
    total = parts_ref[0].astype(jnp.float32)
    for k in range(1, parts_ref.shape[0]):
        total = total + parts_ref[k].astype(jnp.float32)
    total = total.astype(jnp.bfloat16)
    for k in range(out_ref.shape[0]):
        out_ref[k] = total


def apply_kernel(place_ref, packed_ref, normed_ref, scaling_ref, out_ref, up_ref):
    core, group = place_ref[0], place_ref[1]
    mine = [normed_ref[core, i * SIDE : (i + 1) * SIDE] for i in range(BLOCKS)]
    zero = jnp.zeros((1, PART), jnp.float32)
    on_diag = zero
    for i in range(BLOCKS):
        other = normed_ref[1 - core, i * SIDE : (i + 1) * SIDE].astype(jnp.float32)
        on_diag = on_diag + jnp.sum(mine[i].astype(jnp.float32) * other, axis=0, keepdims=True)
    on_diag = on_diag / BATCH
    slope = -2.0 * (1.0 - on_diag) - 2.0 * LAMBDA * on_diag
    squares, first, second = zero, zero, zero
    for i in range(BLOCKS):
        held = mine[i].astype(jnp.float32)
        product = FEATURES * held
        for j in range(BLOCKS):
            if i >= j:
                block = packed_ref[place(i, j) : place(i, j) + SIDE]
                product = product + jnp.dot(block, mine[j], preferred_element_type=jnp.float32)
            else:
                block = packed_ref[place(j, i) : place(j, i) + SIDE]
                product = product + lax.dot_general(
                    block, mine[j], TN, preferred_element_type=jnp.float32
                )
        other = normed_ref[1 - core, i * SIDE : (i + 1) * SIDE].astype(jnp.float32)
        up = (2.0 * LAMBDA / BATCH) * product + slope * other
        up_ref[i * SIDE : (i + 1) * SIDE] = up
        squares = squares + jnp.sum(product * held, axis=0, keepdims=True)
        first = first + jnp.sum(up, axis=0, keepdims=True)
        second = second + jnp.sum(up * held, axis=0, keepdims=True)
    squares, first, second = squares / (BATCH * BATCH), first / BATCH, second / BATCH
    loss = (1.0 - on_diag) * (1.0 - on_diag) + LAMBDA * (squares - on_diag * on_diag)
    scaling = scaling_ref[core]
    for k in range(SLICES):
        for c in range(2):
            start = c * (BATCH // 2) + (group * SLICES + k) * ROWS
            rows = pl.ds(pl.multiple_of(start, ROWS), ROWS)
            held = normed_ref[core, rows].astype(jnp.float32)
            grad = scaling * (up_ref[rows] - first - held * second)
            out_ref[2 * k + c, :ROWS] = grad.astype(jnp.bfloat16)
    high = loss.astype(jnp.bfloat16)
    rest = loss - high.astype(jnp.float32)
    middle = rest.astype(jnp.bfloat16)
    low = (rest - middle.astype(jnp.float32)).astype(jnp.bfloat16)
    index = lax.broadcasted_iota(jnp.int32, (ROWS, PART), 0)
    terms = [jnp.broadcast_to(t.astype(jnp.float32), (ROWS, PART)) for t in (high, middle, low)]
    tail = jnp.where(index == 0, terms[0], jnp.where(index == 1, terms[1], terms[2]))
    tail = tail.astype(jnp.bfloat16)
    for k in range(2 * SLICES):
        out_ref[k, ROWS:] = tail


def unpack_kernel(parts_ref, loss_ref, one_ref, two_ref):
    for k in range(SLICES):
        columns = slice(k * PART, (k + 1) * PART)
        one_ref[:, columns] = parts_ref[2 * k, :ROWS].astype(jnp.float32)
        two_ref[:, columns] = parts_ref[2 * k + 1, :ROWS].astype(jnp.float32)
        tail = parts_ref[2 * k, ROWS:].astype(jnp.float32)
        loss_ref[:, columns] = tail[0:1] + (tail[1:2] + tail[2:3])


def local(view_one, view_two):
    bf16, f32 = jnp.bfloat16, jnp.float32
    shape = jax.ShapeDtypeStruct
    core = lax.axis_index("c").astype(jnp.int32)
    group = lax.axis_index("zh").astype(jnp.int32)
    where = jnp.stack([core, group])

    sent = call(spread_kernel, shape((OWNERS, 2, ROWS, PART), bf16), 0, view_one, view_two)
    whole = lax.all_gather(swap(sent, CHIPS), "c", axis=0, tiled=True)

    normed, scaling, packed = call(
        gram_kernel,
        [shape((2, BATCH, PART), bf16), shape((2, 1, PART), f32), shape((PACKED, SIDE), bf16)],
        2 * BATCH * BATCH * PART,
        where,
        whole,
        scalars=1,
    )
    strips = swap(packed.reshape(OWNERS, CHUNK, SIDE), FEAT)
    strips = swap(call(sum_kernel, shape((SLICES, CHUNK, SIDE), bf16), 0, strips), "zl")
    strips = swap(call(sum_kernel, shape((OWNERS, CHUNK, SIDE), bf16), 0, strips), FEAT)

    out = call(
        apply_kernel,
        shape((2 * SLICES, 2 * ROWS, PART), bf16),
        2 * BATCH * BATCH * PART,
        where,
        strips.reshape(PACKED, SIDE),
        normed,
        scaling,
        scratch=[pltpu.VMEM((BATCH, PART), f32)],
        scalars=1,
    )
    loss, one, two = call(
        unpack_kernel,
        [shape((1, WIDTH), f32), shape((ROWS, WIDTH), f32), shape((ROWS, WIDTH), f32)],
        0,
        swap(out, ("zl", "c")),
    )
    return (loss.reshape(WIDTH), one, two)


def solution(mesh):
    cut = Mesh(mesh.devices.reshape(CUTS), NAMES)
    spread = P(("zh", "zl", "c"), FEAT)
    return jax.shard_map(
        local, mesh=cut, in_specs=(spread, spread), out_specs=(P(FEAT), spread, spread), check_vma=False
    )
```

time: 95.4 us -> 90.2 us (0.945)
  waiting for transfers between devices: 21.9 us -> 13.1 us
  blocking collectives: 46.5 us -> 54.9 us
  Pallas kernels: 0 us -> 3.75 us
  starting transfers between devices: 19.3 us -> 15.7 us
  local copies, waits for them, and re-layouts: 3.99 us -> 1.51 us
  other arithmetic: 1.69 us -> 0.08 us
    all_to_all x2 -> x1, waiting for transfers between devices: 21.9 us -> 13.1 us  [swap(): return lax.all_to_all(values, axes, split_axis=0, concat_axis=0)]
    all_to_all x3 -> x4, blocking collectives: 38.6 us -> 47 us  [swap(): return lax.all_to_all(values, axes, split_axis=0, concat_axis=0)]
    pallas_call x0 -> x6, Pallas kernels: none -> 3.75 us  [call(): pl.pallas_call(kernel, out_shape=out_shape, in_specs=specs, out_specs=[wh...]
    all_to_all x2 -> x1, starting transfers between devices: 19.3 us -> 15.7 us  [swap(): return lax.all_to_all(values, axes, split_axis=0, concat_axis=0)]
    broadcast_in_dim x5 -> x0, local copies, waits for them, and re-layouts: 1.58 us -> none  [the longest x1 0.84 us: local(): jnp.broadcast_to(strip[None], (16,) + strip.shape)]
  transfers between devices with their start and end apart: 2 -> 1, of which waited for: 2 -> 1; matrix products, arithmetic and copies ran while one was open for 0% -> 0% of each run, Pallas kernels for 0% -> 0%
where the time goes in v2:
time: 90.2 us; the launch traced here: 89.7 us
  blocking collectives  54.9 us (61%)
  starting transfers between devices  15.7 us (17%)
  waiting for transfers between devices  13.1 us (15%)
  Pallas kernels  3.75 us (4%)
  local copies, waits for them, and re-layouts  1.51 us (2%)
    all_to_all x4, blocking collectives, swap(): return lax.all_to_all(values, axes, split_axis=0, concat_axis=0)  47 us
    all_to_all x1, starting transfers between devices, swap(): return lax.all_to_all(values, axes, split_axis=0, concat_axis=0)  15.7 us
    all_to_all x1, waiting for transfers between devices, swap(): return lax.all_to_all(values, axes, split_axis=0, concat_axis=0)  13.1 us
    all_gather x1, blocking collectives, local(): whole = lax.all_gather(swap(sent, CHIPS), 'c', axis=0, tiled=True)  7.98 us
    pallas_call x6, Pallas kernels, call(): pl.pallas_call(kernel, out_shape=out_shape, in_specs=specs, out_specs=[wh...  3.75 us
  transfers between devices with their start and end apart: 1, of which 1 were waited for; matrix products, arithmetic and copies ran while one was open for 0% of the time, Pallas kernels for 0%

profile of v2, /device:TPU:1, one launch (start us, length us, event | category | flops | bytes accessed | tf_op | source)
XLA Modules:
  0.0 89.7 jit_solution(3064630135519687165)
XLA Ops:
  0.6 0.0 copy-start
  0.6 0.7 copy-done
  1.4 0.0 copy-start.1
  1.4 0.8 copy-done.1
  2.1 0.7 shard_map.49
  2.9 15.7 %all-to-all-start = ((bf16[16,2,16,256]{3,2,1,0:T(8,128)(2,1)}), bf16[16,2,16,256]{3,2,1,0:T(8,128)(2,1)S(1)}, u32[]{:S(2)}, u32[]{:S(2)}) async-start(bf16[16,2,16,256]{3,2,1,0:T(8,128)(2,1)} %shard_map.49), calls=%async_computation | async-start | bytes 524288 | tf_op jit(solution)/shard_map/all_to_all | solution.py:32
  18.6 0.1 pad_add_fusion.core_ref.place_ref
  18.7 13.1 %all-to-all-done = bf16[16,2,16,256]{3,2,1,0:T(8,128)(2,1)S(1)} async-done(((bf16[16,2,16,256]{3,2,1,0:T(8,128)(2,1)}), bf16[16,2,16,256]{3,2,1,0:T(8,128)(2,1)S(1)}, u32[]{:S(2)}, u32[]{:S(2)}) %all-to-all-start) | async-done | bytes 262176 | tf_op jit(solution)/shard_map/all_to_all | solution.py:32
  31.8 8.0 %all_gather.3.whole_ref = bf16[32,2,16,256]{3,2,1,0:T(8,128)(2,1)S(1)} all-gather(bf16[16,2,16,256]{3,2,1,0:T(8,128)(2,1)S(1)} %all-to-all-done), channel_id=1, replica_groups=mesh['zh'=4,'zl'=4,'c'=2,'y'=4,'x'=4] {'c'}, dimensions={0}, use_global_device_ids=true | all-gather | bytes 786432 | tf_op jit(solution)/shard_map/all_gather | solution.py:165
  39.7 1.2 %shard_map.50 = (bf16[2,512,256]{2,1,0:T(8,128)(2,1)S(1)}, f32[2,1,256]{2,1,0:T(1,128)S(1)}, bf16[1280,128]{1,0:T(8,128)(2,1)S(1)}) custom-call(s32[2]{0:T(128)S(1)} %pad_add_fusion.core_ref.place_ref, bf16[32,2,16,256]{3,2,1,0:T(8,128)(2,1)S(1)} %all_gather.3.whole_ref), custom_call_target="tpu_custom_call" | custom-call | flops 134217728 | bytes 524296 | tf_op jit(solution)/shard_map/pallas_call | solution.py:45
  41.0 15.4 %all_to_all.25.parts_ref = bf16[16,80,128]{2,1,0:T(8,128)(2,1)S(1)} all-to-all(bf16[16,80,128]{2,1,0:T(8,128)(2,1)S(1)} %bitcast.6), channel_id=1, replica_groups=mesh['zh'=4,'zl'=4,'c'=2,'y'=4,'x'=4] {'y','x'}, dimensions={0} | all-to-all | bytes 655360 | tf_op jit(solution)/shard_map/all_to_all | solution.py:32
  56.4 8.5 %all_to_all.26.parts_ref = bf16[4,80,128]{2,1,0:T(8,128)(2,1)S(1)} all-to-all(bf16[4,80,128]{2,1,0:T(8,128)(2,1)S(1)} %shard_map.51), channel_id=1, replica_groups=mesh['zh'=4,'zl'=4,'c'=2,'y'=4,'x'=4] {'zl'}, dimensions={0} | all-to-all | bytes 163840 | tf_op jit(solution)/shard_map/all_to_all | solution.py:32
  65.0 10.9 %all_to_all.27 = bf16[16,80,128]{2,1,0:T(8,128)(2,1)S(1)} all-to-all(bf16[16,80,128]{2,1,0:T(8,128)(2,1)S(1)} %shard_map.52), channel_id=1, replica_groups=mesh['zh'=4,'zl'=4,'c'=2,'y'=4,'x'=4] {'y','x'}, dimensions={0} | all-to-all | bytes 655360 | tf_op jit(solution)/shard_map/all_to_all | solution.py:32
  75.8 1.1 %shard_map.53 = bf16[8,32,256]{2,1,0:T(8,128)(2,1)S(1)} custom-call(s32[2]{0:T(128)S(1)} %pad_add_fusion.core_ref.place_ref, bf16[1280,128]{1,0:T(8,128)(2,1)S(1)} %bitcast.5, bf16[2,512,256]{2,1,0:T(8,128)(2,1)S(1)} %get-tuple-element.10.normed_ref, f32[2,1,256]{2,1,0:T(1,128)S(1)} %get-tuple-element.11.scaling_ref), custom_call_target="tpu_custom_call" | custom-call | flops 134217728 | bytes 854024 | tf_op jit(solution)/shard_map/pallas_call | solution.py:45
  76.9 12.2 %all_to_all.28.parts_ref = bf16[8,32,256]{2,1,0:T(8,128)(2,1)S(1)} all-to-all(bf16[8,32,256]{2,1,0:T(8,128)(2,1)S(1)} %shard_map.53), channel_id=1, replica_groups=mesh['zh'=4,'zl'=4,'c'=2,'y'=4,'x'=4] {'zl','c'}, dimensions={0} | all-to-all | bytes 262144 | tf_op jit(solution)/shard_map/all_to_all | solution.py:32
  89.1 0.7 shard_map.54
  (2 shorter events, 0.1 us)
Async XLA Ops:
  0.6 0.8 copy-start
  1.4 0.8 copy-start.1
  2.9 28.9 %all-to-all-start = ((bf16[16,2,16,256]{3,2,1,0:T(8,128)(2,1)}), bf16[16,2,16,256]{3,2,1,0:T(8,128)(2,1)S(1)}, u32[]{:S(2)}, u32[]{:S(2)}) async-start(bf16[16,2,16,256]{3,2,1,0:T(8,128)(2,1)} %shard_map.49), calls=%async_computation | async-start | bytes 524288 | tf_op jit(solution)/shard_map/all_to_all | solution.py:32

commit v3 on v2

v3 whole, which is shorter than its diff:
```python
import jax
import jax.numpy as jnp
from jax import lax
from jax.experimental import pallas as pl
from jax.experimental.pallas import tpu as pltpu
from jax.sharding import Mesh, PartitionSpec as P

EPSILON = 1e-05
LAMBDA = 0.0051
FEATURES = 16384
BATCH = 512

CUTS = (4, 4, 2, 4, 4)
NAMES = ("zh", "zl", "c", "y", "x")
IMAGES = ("zh", "zl", "c")
FEAT = ("y", "x")
GROUPS = 4
SLICES = 4
OWNERS = 16
ROWS = 16
WIDTH = 1024
PART = WIDTH // SLICES
SIDE = 128
BLOCKS = BATCH // SIDE
PACKED = BLOCKS * (BLOCKS + 1) // 2 * SIDE
CHUNK = PACKED // OWNERS
NT = (((1,), (1,)), ((), ()))
TN = (((0,), (0,)), ((), ()))


def swap(values, axes):
    return lax.all_to_all(values, axes, split_axis=0, concat_axis=0)


def place(i, j):
    return (i * (i + 1) // 2 + j) * SIDE


def call(kernel, out_shape, flops, *operands, scratch=(), scalars=0):
    moved = sum(o.size * o.dtype.itemsize for o in operands)
    specs = [pl.BlockSpec(memory_space=pltpu.SMEM)] * scalars
    specs += [pl.BlockSpec(memory_space=pltpu.VMEM)] * (len(operands) - scalars)
    many = isinstance(out_shape, (list, tuple))
    whole = pl.BlockSpec(memory_space=pltpu.VMEM)
    return pl.pallas_call(
        kernel,
        out_shape=out_shape,
        in_specs=specs,
        out_specs=[whole] * len(out_shape) if many else whole,
        scratch_shapes=list(scratch),
        cost_estimate=pl.CostEstimate(flops=flops, bytes_accessed=moved, transcendentals=0),
        compiler_params=pltpu.CompilerParams(vmem_limit_bytes=16 * 1024 * 1024),
    )(*operands)


def spread_kernel(one_ref, two_ref, out_ref, held_ref, sems):
    refs = (one_ref, two_ref)
    copies = [pltpu.make_async_copy(refs[v], held_ref.at[v], sems.at[v]) for v in range(2)]
    for copy in copies:
        copy.start()
    for v in range(2):
        copies[v].wait()
        for k in range(SLICES):
            piece = held_ref[v, :, k * PART : (k + 1) * PART]
            for h in range(GROUPS):
                out_ref[(h * SLICES + k) * 2 + 1 - v] = piece


def normalize(values):
    values = values.astype(jnp.float32)
    center = jnp.sum(values, axis=0, keepdims=True) / BATCH
    shifted = values - center
    spread = jnp.sum(shifted * shifted, axis=0, keepdims=True) / BATCH
    scaling = lax.rsqrt(spread + EPSILON)
    return (shifted * scaling).astype(jnp.bfloat16), scaling


def gram_kernel(raw_ref, other_ref, packed_ref):
    other_ref[...], _ = normalize(raw_ref[...])
    row = lax.broadcasted_iota(jnp.int32, (SIDE, SIDE), 0)
    column = lax.broadcasted_iota(jnp.int32, (SIDE, SIDE), 1)
    mean_diag = jnp.where(row == column, float(PART), 0.0)
    for i in range(BLOCKS):
        left = other_ref[i * SIDE : (i + 1) * SIDE]
        for j in range(i + 1):
            right = other_ref[j * SIDE : (j + 1) * SIDE]
            block = lax.dot_general(left, right, NT, preferred_element_type=jnp.float32)
            if i == j:
                block = block - mean_diag
            packed_ref[place(i, j) : place(i, j) + SIDE] = block.astype(jnp.bfloat16)


def mine_kernel(raw_ref, other_ref, mine_ref, terms_ref):
    mine_ref[...], scaling = normalize(raw_ref[...])
    both = mine_ref[...].astype(jnp.float32) * other_ref[...].astype(jnp.float32)
    on_diag = jnp.sum(both, axis=0, keepdims=True) / BATCH
    terms_ref[0:1] = scaling
    terms_ref[1:2] = on_diag
    terms_ref[2:3] = -2.0 * (1.0 - on_diag) - 2.0 * LAMBDA * on_diag


def sum_kernel(parts_ref, out_ref):
    total = parts_ref[0].astype(jnp.float32)
    for k in range(1, parts_ref.shape[0]):
        total = total + parts_ref[k].astype(jnp.float32)
    total = total.astype(jnp.bfloat16)
    for k in range(out_ref.shape[0]):
        out_ref[k] = total


def apply_kernel(place_ref, packed_ref, mine_ref, other_ref, terms_ref, out_ref, up_ref):
    group = place_ref[0]
    mine = [mine_ref[i * SIDE : (i + 1) * SIDE] for i in range(BLOCKS)]
    scaling, on_diag, slope = terms_ref[0:1], terms_ref[1:2], terms_ref[2:3]
    zero = jnp.zeros((1, PART), jnp.float32)
    squares, first, second = zero, zero, zero
    for i in range(BLOCKS):
        held = mine[i].astype(jnp.float32)
        product = FEATURES * held
        for j in range(BLOCKS):
            if i >= j:
                block = packed_ref[place(i, j) : place(i, j) + SIDE]
                product = product + jnp.dot(block, mine[j], preferred_element_type=jnp.float32)
            else:
                block = packed_ref[place(j, i) : place(j, i) + SIDE]
                product = product + lax.dot_general(
                    block, mine[j], TN, preferred_element_type=jnp.float32
                )
        other = other_ref[i * SIDE : (i + 1) * SIDE].astype(jnp.float32)
        up = (2.0 * LAMBDA / BATCH) * product + slope * other
        up_ref[i * SIDE : (i + 1) * SIDE] = up
        squares = squares + jnp.sum(product * held, axis=0, keepdims=True)
        first = first + jnp.sum(up, axis=0, keepdims=True)
        second = second + jnp.sum(up * held, axis=0, keepdims=True)
    squares, first, second = squares / (BATCH * BATCH), first / BATCH, second / BATCH
    loss = (1.0 - on_diag) * (1.0 - on_diag) + LAMBDA * (squares - on_diag * on_diag)
    for k in range(SLICES):
        for c in range(2):
            start = ((group * SLICES + k) * 2 + c) * ROWS
            rows = pl.ds(pl.multiple_of(start, ROWS), ROWS)
            held = mine_ref[rows].astype(jnp.float32)
            grad = scaling * (up_ref[rows] - first - held * second)
            out_ref[2 * k + c, :, :PART] = grad.astype(jnp.bfloat16)
    high = loss.astype(jnp.bfloat16)
    rest = loss - high.astype(jnp.float32)
    middle = rest.astype(jnp.bfloat16)
    low = (rest - middle.astype(jnp.float32)).astype(jnp.bfloat16)
    index = lax.broadcasted_iota(jnp.int32, (ROWS, SIDE), 0)
    tail = jnp.zeros((ROWS, SIDE), jnp.float32)
    for n, term in enumerate((high, middle, low)):
        for half in range(PART // SIDE):
            row = term[:, half * SIDE : (half + 1) * SIDE].astype(jnp.float32)
            tail = jnp.where(index == n * (PART // SIDE) + half, row, tail)
    tail = tail.astype(jnp.bfloat16)
    for k in range(2 * SLICES):
        out_ref[k, :, PART:] = tail


def unpack_kernel(parts_ref, loss_ref, one_ref, two_ref):
    halves = PART // SIDE
    for k in range(SLICES):
        columns = slice(k * PART, (k + 1) * PART)
        one_ref[:, columns] = parts_ref[2 * k, :, :PART].astype(jnp.float32)
        two_ref[:, columns] = parts_ref[2 * k + 1, :, :PART].astype(jnp.float32)
        tail = parts_ref[2 * k, :, PART:].astype(jnp.float32)
        for half in range(halves):
            high, middle, low = [tail[n * halves + half : n * halves + half + 1] for n in range(3)]
            start = k * PART + half * SIDE
            loss_ref[:, start : start + SIDE] = high + (middle + low)


def local(view_one, view_two):
    bf16, f32 = jnp.bfloat16, jnp.float32
    shape = jax.ShapeDtypeStruct
    group = lax.axis_index("zh").astype(jnp.int32).reshape(1)

    sent = pl.pallas_call(
        spread_kernel,
        out_shape=pltpu.VMEM((2 * OWNERS, ROWS, PART), bf16),
        in_specs=[pl.BlockSpec(memory_space=pl.ANY)] * 2,
        out_specs=pl.BlockSpec(memory_space=pltpu.VMEM),
        scratch_shapes=[pltpu.VMEM((2, ROWS, WIDTH), bf16), pltpu.SemaphoreType.DMA((2,))],
    )(view_one, view_two)
    raw = swap(sent, IMAGES).reshape(BATCH, PART)
    raw_mine = lax.ppermute(raw, "c", [(0, 1), (1, 0)])

    other, packed = call(
        gram_kernel,
        [shape((BATCH, PART), bf16), shape((PACKED, SIDE), bf16)],
        2 * BATCH * BATCH * PART,
        raw,
    )
    mine, terms = call(
        mine_kernel, [shape((BATCH, PART), bf16), shape((8, PART), f32)], 0, raw_mine, other
    )
    strips = swap(packed.reshape(OWNERS, CHUNK, SIDE), FEAT)
    strips = swap(call(sum_kernel, shape((SLICES, CHUNK, SIDE), bf16), 0, strips), "zl")
    strips = swap(call(sum_kernel, shape((OWNERS, CHUNK, SIDE), bf16), 0, strips), FEAT)

    out = call(
        apply_kernel,
        shape((2 * SLICES, ROWS, PART + SIDE), bf16),
        2 * BATCH * BATCH * PART,
        group,
        strips.reshape(PACKED, SIDE),
        mine,
        other,
        terms,
        scratch=[pltpu.VMEM((BATCH, PART), f32)],
        scalars=1,
    )
    loss, one, two = call(
        unpack_kernel,
        [shape((1, WIDTH), f32), shape((ROWS, WIDTH), f32), shape((ROWS, WIDTH), f32)],
        0,
        swap(out, ("zl", "c")),
    )
    return (loss.reshape(WIDTH), one, two)


def solution(mesh):
    cut = Mesh(mesh.devices.reshape(CUTS), NAMES)
    spread = P(IMAGES, FEAT)
    return jax.shard_map(
        local, mesh=cut, in_specs=(spread, spread), out_specs=(P(FEAT), spread, spread), check_vma=False
    )
```

time: 90.2 us -> 88.4 us (0.980)
  blocking collectives: 54.9 us -> 72.6 us
  waiting for transfers between devices: 13.1 us -> 3.17 us
  starting transfers between devices: 15.7 us -> 8 us
  local copies, waits for them, and re-layouts: 1.51 us -> 0 us
    all_to_all x4, blocking collectives: 47 us -> 72.6 us  [swap(): return lax.all_to_all(values, axes, split_axis=0, concat_axis=0)]
    all_to_all x1, starting transfers between devices: 15.7 us -> 3.54 us  [swap(): return lax.all_to_all(values, axes, split_axis=0, concat_axis=0)]
    all_to_all x1, waiting for transfers between devices: 13.1 us -> 2.04 us  [swap(): return lax.all_to_all(values, axes, split_axis=0, concat_axis=0)]
    all_gather x1 -> x0, blocking collectives: 7.98 us -> none  [local(): whole = lax.all_gather(swap(sent, CHIPS), 'c', axis=0, tiled=True)]
    ppermute x0 -> x1, starting transfers between devices: none -> 4.46 us  [local(): raw_mine = lax.ppermute(raw, 'c', [(0, 1), (1, 0)])]
    unnamed x4 -> x0, local copies, waits for them, and re-layouts: 1.51 us -> none
    ppermute x0 -> x1, waiting for transfers between devices: none -> 1.14 us  [local(): raw_mine = lax.ppermute(raw, 'c', [(0, 1), (1, 0)])]
    pallas_call x6, Pallas kernels: 3.75 us -> 2.7 us  [call(): pl.pallas_call(kernel, out_shape=out_shape, in_specs=specs, out_specs=[wh...]
  transfers between devices with their start and end apart: 1 -> 2, of which waited for: 1 -> 2; matrix products, arithmetic and copies ran while one was open for 0% -> 0% of each run, Pallas kernels for 0% -> 0%
where the time goes in v3:
time: 88.4 us; the launch traced here: 88 us
  blocking collectives  72.6 us (82%)
  starting transfers between devices  8 us (9%)
  Pallas kernels  3.51 us (4%)
  waiting for transfers between devices  3.17 us (4%)
    all_to_all x4, blocking collectives, swap(): return lax.all_to_all(values, axes, split_axis=0, concat_axis=0)  72.6 us
    ppermute x1, starting transfers between devices, local(): raw_mine = lax.ppermute(raw, 'c', [(0, 1), (1, 0)])  4.46 us
    all_to_all x1, starting transfers between devices, swap(): return lax.all_to_all(values, axes, split_axis=0, concat_axis=0)  3.54 us
    pallas_call x6, Pallas kernels, call(): pl.pallas_call(kernel, out_shape=out_shape, in_specs=specs, out_specs=[wh...  2.7 us
    all_to_all x1, waiting for transfers between devices, swap(): return lax.all_to_all(values, axes, split_axis=0, concat_axis=0)  2.04 us
  transfers between devices with their start and end apart: 2, of which 2 were waited for; matrix products, arithmetic and copies ran while one was open for 0% of the time, Pallas kernels for 0%

profile of v3, /device:TPU:1, one launch (start us, length us, event | category | flops | bytes accessed | tf_op | source)
XLA Modules:
  0.0 88.0 jit_solution(11894682019260735158)
XLA Ops:
  0.6 0.8 shard_map.49
  1.4 38.5 %all_to_all.25 = bf16[32,16,256]{2,1,0:T(8,128)(2,1)S(1)} all-to-all(bf16[32,16,256]{2,1,0:T(8,128)(2,1)S(1)} %shard_map.49), channel_id=1, replica_groups=mesh['zh'=4,'zl'=4,'c'=2,'y'=4,'x'=4] {'zh','zl','c'}, dimensions={0} | all-to-all | bytes 524288 | tf_op jit(solution)/shard_map/all_to_all | solution.py:32
  40.0 0.5 shard_map.50
  40.5 14.6 %all_to_all.26.parts_ref = bf16[16,80,128]{2,1,0:T(8,128)(2,1)S(1)} all-to-all(bf16[16,80,128]{2,1,0:T(8,128)(2,1)S(1)} %bitcast.6), channel_id=1, replica_groups=mesh['zh'=4,'zl'=4,'c'=2,'y'=4,'x'=4] {'y','x'}, dimensions={0} | all-to-all | bytes 655360 | tf_op jit(solution)/shard_map/all_to_all | solution.py:32
  55.2 7.9 %all_to_all.27.parts_ref = bf16[4,80,128]{2,1,0:T(8,128)(2,1)S(1)} all-to-all(bf16[4,80,128]{2,1,0:T(8,128)(2,1)S(1)} %shard_map.51), channel_id=1, replica_groups=mesh['zh'=4,'zl'=4,'c'=2,'y'=4,'x'=4] {'zl'}, dimensions={0} | all-to-all | bytes 163840 | tf_op jit(solution)/shard_map/all_to_all | solution.py:32
  63.1 0.7 shard_map.52
  63.8 3.5 %all-to-all-start.3 = ((bf16[16,80,128]{2,1,0:T(8,128)(2,1)}), bf16[16,80,128]{2,1,0:T(8,128)(2,1)S(1)}, u32[]{:S(2)}, u32[]{:S(2)}) async-start(bf16[16,80,128]{2,1,0:T(8,128)(2,1)} %shard_map.52), calls=%async_computation.3 | async-start | bytes 655360 | tf_op jit(solution)/shard_map/all_to_all | solution.py:32
  67.4 4.5 %collective-permute-start = (bf16[512,256]{1,0:T(8,128)(2,1)S(1)}, bf16[512,256]{1,0:T(8,128)(2,1)S(1)}, u32[]{:S(2)}, u32[]{:S(2)}) collective-permute-start(bf16[512,256]{1,0:T(8,128)(2,1)S(1)} %bitcast.8), channel_id=1, source_target_pairs={{0,16},{16,0},{1,17},{17,1},{2,18},{18,2},{3,19},{19,3},{4,20},{20... | collective-permute-start | bytes 786440 | tf_op jit(solution)/shard_map/ppermute | solution.py:185
  71.8 1.1 %collective-permute-done.raw_ref = bf16[512,256]{1,0:T(8,128)(2,1)S(1)} collective-permute-done((bf16[512,256]{1,0:T(8,128)(2,1)S(1)}, bf16[512,256]{1,0:T(8,128)(2,1)S(1)}, u32[]{:S(2)}, u32[]{:S(2)}) %collective-permute-start) | collective-permute-done | bytes 262176 | tf_op jit(solution)/shard_map/ppermute | solution.py:185
  73.0 0.2 shard_map.53
  73.2 2.0 %all-to-all-done.3 = bf16[16,80,128]{2,1,0:T(8,128)(2,1)S(1)} async-done(((bf16[16,80,128]{2,1,0:T(8,128)(2,1)}), bf16[16,80,128]{2,1,0:T(8,128)(2,1)S(1)}, u32[]{:S(2)}, u32[]{:S(2)}) %all-to-all-start.3) | async-done | bytes 327712 | tf_op jit(solution)/shard_map/all_to_all | solution.py:32
  75.2 0.5 shard_map.54
  75.7 11.6 %all_to_all.28.parts_ref = bf16[8,16,384]{2,1,0:T(8,128)(2,1)S(1)} all-to-all(bf16[8,16,384]{2,1,0:T(8,128)(2,1)S(1)} %shard_map.54), channel_id=1, replica_groups=mesh['zh'=4,'zl'=4,'c'=2,'y'=4,'x'=4] {'zl','c'}, dimensions={0} | all-to-all | bytes 196608 | tf_op jit(solution)/shard_map/all_to_all | solution.py:32
  87.3 0.7 shard_map.55
  (1 shorter events, 0.0 us)
Async XLA Ops:
  63.8 11.4 %all-to-all-start.3 = ((bf16[16,80,128]{2,1,0:T(8,128)(2,1)}), bf16[16,80,128]{2,1,0:T(8,128)(2,1)S(1)}, u32[]{:S(2)}, u32[]{:S(2)}) async-start(bf16[16,80,128]{2,1,0:T(8,128)(2,1)} %shard_map.52), calls=%async_computation.3 | async-start | bytes 655360 | tf_op jit(solution)/shard_map/all_to_all | solution.py:32
  67.4 5.6 %collective-permute-start = (bf16[512,256]{1,0:T(8,128)(2,1)S(1)}, bf16[512,256]{1,0:T(8,128)(2,1)S(1)}, u32[]{:S(2)}, u32[]{:S(2)}) collective-permute-start(bf16[512,256]{1,0:T(8,128)(2,1)S(1)} %bitcast.8), channel_id=1, source_target_pairs={{0,16},{16,0},{1,17},{17,1},{2,18},{18,2},{3,19},{19,3},{4,20},{20... | collective-permute-start | bytes 786440 | tf_op jit(solution)/shard_map/ppermute | solution.py:185

commit v4 on v3

--- a/solution.py
+++ b/solution.py
@@ -10,9 +10,10 @@
 FEATURES = 16384
 BATCH = 512
 
-CUTS = (4, 4, 2, 4, 4)
-NAMES = ("zh", "zl", "c", "y", "x")
-IMAGES = ("zh", "zl", "c")
+CUTS = (2, 2, 2, 2, 2, 4, 4)
+NAMES = ("a", "b", "e", "d", "c", "y", "x")
+IMAGES = ('b', 'e', 'd', 'a', 'c')
+NEAR = ("e", "d")
 FEAT = ("y", "x")
 GROUPS = 4
 SLICES = 4
@@ -53,6 +54,10 @@
     )(*operands)
 
 
+def position(h, k, c):
+    return (h % 2) * 16 + (k // 2) * 8 + (k % 2) * 4 + (h // 2) * 2 + (c) * 1
+
+
 def spread_kernel(one_ref, two_ref, out_ref, held_ref, sems):
     refs = (one_ref, two_ref)
     copies = [pltpu.make_async_copy(refs[v], held_ref.at[v], sems.at[v]) for v in range(2)]
@@ -63,7 +68,7 @@
         for k in range(SLICES):
             piece = held_ref[v, :, k * PART : (k + 1) * PART]
             for h in range(GROUPS):
-                out_ref[(h * SLICES + k) * 2 + 1 - v] = piece
+                out_ref[position(h, k, 1 - v)] = piece
 
 
 def normalize(values):
@@ -136,7 +141,7 @@
     loss = (1.0 - on_diag) * (1.0 - on_diag) + LAMBDA * (squares - on_diag * on_diag)
     for k in range(SLICES):
         for c in range(2):
-            start = ((group * SLICES + k) * 2 + c) * ROWS
+            start = position(group, k, c) * ROWS
             rows = pl.ds(pl.multiple_of(start, ROWS), ROWS)
             held = mine_ref[rows].astype(jnp.float32)
             grad = scaling * (up_ref[rows] - first - held * second)
@@ -172,7 +177,7 @@
 def local(view_one, view_two):
     bf16, f32 = jnp.bfloat16, jnp.float32
     shape = jax.ShapeDtypeStruct
-    group = lax.axis_index("zh").astype(jnp.int32).reshape(1)
+    group = (lax.axis_index("a") * 2 + lax.axis_index("b")).astype(jnp.int32).reshape(1)
 
     sent = pl.pallas_call(
         spread_kernel,
@@ -194,7 +199,7 @@
         mine_kernel, [shape((BATCH, PART), bf16), shape((8, PART), f32)], 0, raw_mine, other
     )
     strips = swap(packed.reshape(OWNERS, CHUNK, SIDE), FEAT)
-    strips = swap(call(sum_kernel, shape((SLICES, CHUNK, SIDE), bf16), 0, strips), "zl")
+    strips = swap(call(sum_kernel, shape((SLICES, CHUNK, SIDE), bf16), 0, strips), ("d", "e"))
     strips = swap(call(sum_kernel, shape((OWNERS, CHUNK, SIDE), bf16), 0, strips), FEAT)
 
     out = call(
@@ -213,14 +218,14 @@
         unpack_kernel,
         [shape((1, WIDTH), f32), shape((ROWS, WIDTH), f32), shape((ROWS, WIDTH), f32)],
         0,
-        swap(out, ("zl", "c")),
+        swap(out, ("e", "d", "c")),
     )
     return (loss.reshape(WIDTH), one, two)
 
 
 def solution(mesh):
     cut = Mesh(mesh.devices.reshape(CUTS), NAMES)
-    spread = P(IMAGES, FEAT)
+    spread = P(NAMES[:5], FEAT)
     return jax.shard_map(
         local, mesh=cut, in_specs=(spread, spread), out_specs=(P(FEAT), spread, spread), check_vma=False
     )

time: 88.4 us -> 86.3 us (0.976)
  blocking collectives: 72.6 us -> 70.3 us
  waiting for transfers between devices: 3.17 us -> 4.59 us
  starting transfers between devices: 8 us -> 6.73 us
    all_to_all x4, blocking collectives: 72.6 us -> 70.3 us  [swap(): return lax.all_to_all(values, axes, split_axis=0, concat_axis=0)]
    all_to_all x1, waiting for transfers between devices: 2.04 us -> 3.46 us  [swap(): return lax.all_to_all(values, axes, split_axis=0, concat_axis=0)]
    ppermute x1, starting transfers between devices: 4.46 us -> 3.19 us  [local(): raw_mine = lax.ppermute(raw, 'c', [(0, 1), (1, 0)])]
where the time goes in v4:
time: 86.3 us; the launch traced here: 85.9 us
  blocking collectives  70.3 us (81%)
  starting transfers between devices  6.73 us (8%)
  waiting for transfers between devices  4.59 us (5%)
  Pallas kernels  3.5 us (4%)
    all_to_all x4, blocking collectives, swap(): return lax.all_to_all(values, axes, split_axis=0, concat_axis=0)  70.3 us
    all_to_all x1, starting transfers between devices, swap(): return lax.all_to_all(values, axes, split_axis=0, concat_axis=0)  3.54 us
    all_to_all x1, waiting for transfers between devices, swap(): return lax.all_to_all(values, axes, split_axis=0, concat_axis=0)  3.46 us
    ppermute x1, starting transfers between devices, local(): raw_mine = lax.ppermute(raw, 'c', [(0, 1), (1, 0)])  3.19 us
    pallas_call x6, Pallas kernels, call(): pl.pallas_call(kernel, out_shape=out_shape, in_specs=specs, out_specs=[wh...  2.7 us
  transfers between devices with their start and end apart: 2, of which 2 were waited for; matrix products, arithmetic and copies ran while one was open for 0% of the time, Pallas kernels for 0%

profile of v4, /device:TPU:1, one launch (start us, length us, event | category | flops | bytes accessed | tf_op | source)
XLA Modules:
  0.0 85.9 jit_solution(14840138905277791859)
XLA Ops:
  0.6 0.8 shard_map.49
  1.4 35.7 %all_to_all.25 = bf16[32,16,256]{2,1,0:T(8,128)(2,1)S(1)} all-to-all(bf16[32,16,256]{2,1,0:T(8,128)(2,1)S(1)} %shard_map.49), channel_id=1, replica_groups=mesh['a'=2,'b'=2,'e'=2,'d'=2,'c'=2,'y'=4,'x'=4] {'b','e','d','a','c'}, dimensions={0} | all-to-all | bytes 524288 | tf_op jit(solution)/shard_map/all_to_all | solution.py:33
  37.1 0.5 shard_map.50
  37.6 15.4 %all_to_all.26.parts_ref = bf16[16,80,128]{2,1,0:T(8,128)(2,1)S(1)} all-to-all(bf16[16,80,128]{2,1,0:T(8,128)(2,1)S(1)} %bitcast.6), channel_id=1, replica_groups=mesh['a'=2,'b'=2,'e'=2,'d'=2,'c'=2,'y'=4,'x'=4] {'y','x'}, dimensions={0} | all-to-all | bytes 655360 | tf_op jit(solution)/shard_map/all_to_all | solution.py:33
  53.0 9.1 %all_to_all.27.parts_ref = bf16[4,80,128]{2,1,0:T(8,128)(2,1)S(1)} all-to-all(bf16[4,80,128]{2,1,0:T(8,128)(2,1)S(1)} %shard_map.51), channel_id=1, replica_groups=mesh['a'=2,'b'=2,'e'=2,'d'=2,'c'=2,'y'=4,'x'=4] {'d','e'}, dimensions={0} | all-to-all | bytes 163840 | tf_op jit(solution)/shard_map/all_to_all | solution.py:33
  62.2 0.7 shard_map.52
  62.9 3.5 %all-to-all-start.3 = ((bf16[16,80,128]{2,1,0:T(8,128)(2,1)}), bf16[16,80,128]{2,1,0:T(8,128)(2,1)S(1)}, u32[]{:S(2)}, u32[]{:S(2)}) async-start(bf16[16,80,128]{2,1,0:T(8,128)(2,1)} %shard_map.52), calls=%async_computation.3 | async-start | bytes 655360 | tf_op jit(solution)/shard_map/all_to_all | solution.py:33
  66.5 3.2 %collective-permute-start = (bf16[512,256]{1,0:T(8,128)(2,1)S(1)}, bf16[512,256]{1,0:T(8,128)(2,1)S(1)}, u32[]{:S(2)}, u32[]{:S(2)}) collective-permute-start(bf16[512,256]{1,0:T(8,128)(2,1)S(1)} %bitcast.8), channel_id=1, source_target_pairs={{0,16},{16,0},{1,17},{17,1},{2,18},{18,2},{3,19},{19,3},{4,20},{20... | collective-permute-start | bytes 786440 | tf_op jit(solution)/shard_map/ppermute | solution.py:190
  69.7 1.1 %collective-permute-done.raw_ref = bf16[512,256]{1,0:T(8,128)(2,1)S(1)} collective-permute-done((bf16[512,256]{1,0:T(8,128)(2,1)S(1)}, bf16[512,256]{1,0:T(8,128)(2,1)S(1)}, u32[]{:S(2)}, u32[]{:S(2)}) %collective-permute-start) | collective-permute-done | bytes 262176 | tf_op jit(solution)/shard_map/ppermute | solution.py:190
  70.8 0.2 shard_map.53
  71.0 3.5 %all-to-all-done.3 = bf16[16,80,128]{2,1,0:T(8,128)(2,1)S(1)} async-done(((bf16[16,80,128]{2,1,0:T(8,128)(2,1)}), bf16[16,80,128]{2,1,0:T(8,128)(2,1)S(1)}, u32[]{:S(2)}, u32[]{:S(2)}) %all-to-all-start.3) | async-done | bytes 327712 | tf_op jit(solution)/shard_map/all_to_all | solution.py:33
  74.5 0.5 shard_map.54
  75.0 10.2 %all_to_all.28.parts_ref = bf16[8,16,384]{2,1,0:T(8,128)(2,1)S(1)} all-to-all(bf16[8,16,384]{2,1,0:T(8,128)(2,1)S(1)} %shard_map.54), channel_id=1, replica_groups=mesh['a'=2,'b'=2,'e'=2,'d'=2,'c'=2,'y'=4,'x'=4] {'e','d','c'}, dimensions={0} | all-to-all | bytes 196608 | tf_op jit(solution)/shard_map/all_to_all | solution.py:33
  85.2 0.7 shard_map.55
  (1 shorter events, 0.0 us)
Async XLA Ops:
  62.9 11.6 %all-to-all-start.3 = ((bf16[16,80,128]{2,1,0:T(8,128)(2,1)}), bf16[16,80,128]{2,1,0:T(8,128)(2,1)S(1)}, u32[]{:S(2)}, u32[]{:S(2)}) async-start(bf16[16,80,128]{2,1,0:T(8,128)(2,1)} %shard_map.52), calls=%async_computation.3 | async-start | bytes 655360 | tf_op jit(solution)/shard_map/all_to_all | solution.py:33
  66.5 4.3 %collective-permute-start = (bf16[512,256]{1,0:T(8,128)(2,1)S(1)}, bf16[512,256]{1,0:T(8,128)(2,1)S(1)}, u32[]{:S(2)}, u32[]{:S(2)}) collective-permute-start(bf16[512,256]{1,0:T(8,128)(2,1)S(1)} %bitcast.8), channel_id=1, source_target_pairs={{0,16},{16,0},{1,17},{17,1},{2,18},{18,2},{3,19},{19,3},{4,20},{20... | collective-permute-start | bytes 786440 | tf_op jit(solution)/shard_map/ppermute | solution.py:190

commit v5 on v3

--- a/solution.py
+++ b/solution.py
@@ -3,17 +3,14 @@
 from jax import lax
 from jax.experimental import pallas as pl
 from jax.experimental.pallas import tpu as pltpu
-from jax.sharding import Mesh, PartitionSpec as P
+from jax.sharding import PartitionSpec as P
 
 EPSILON = 1e-05
 LAMBDA = 0.0051
 FEATURES = 16384
 BATCH = 512
 
-CUTS = (4, 4, 2, 4, 4)
-NAMES = ("zh", "zl", "c", "y", "x")
-IMAGES = ("zh", "zl", "c")
-FEAT = ("y", "x")
+CHIPS = (0, 4, 2, 6, 1, 5, 3, 7, 8, 12, 10, 14, 9, 13, 11, 15)
 GROUPS = 4
 SLICES = 4
 OWNERS = 16
@@ -28,8 +25,14 @@
 TN = (((0,), (0,)), ((), ()))
 
 
-def swap(values, axes):
-    return lax.all_to_all(values, axes, split_axis=0, concat_axis=0)
+SAME_CORE = [[2 * z + c for z in CHIPS] for c in range(2)]
+CORES = [[2 * z, 2 * z + 1] for z in range(16)]
+NEAR = [[8 * h + 2 * k + c for k in (0, 2, 1, 3)] for h in range(4) for c in range(2)]
+GROUP = [list(range(8 * h, 8 * h + 8)) for h in range(4)]
+
+
+def swap(values, axis, groups=None):
+    return lax.all_to_all(values, axis, split_axis=0, concat_axis=0, axis_index_groups=groups)
 
 
 def place(i, j):
@@ -63,7 +66,7 @@
         for k in range(SLICES):
             piece = held_ref[v, :, k * PART : (k + 1) * PART]
             for h in range(GROUPS):
-                out_ref[(h * SLICES + k) * 2 + 1 - v] = piece
+                out_ref[CHIPS.index(h * SLICES + k), v] = piece
 
 
 def normalize(values):
@@ -75,8 +78,9 @@
     return (shifted * scaling).astype(jnp.bfloat16), scaling
 
 
-def gram_kernel(raw_ref, other_ref, packed_ref):
-    other_ref[...], _ = normalize(raw_ref[...])
+def gram_kernel(core_ref, whole_ref, mine_ref, other_ref, terms_ref, packed_ref):
+    core = core_ref[0]
+    other_ref[...], _ = normalize(whole_ref[:, :, 1 - core].reshape(BATCH, PART))
     row = lax.broadcasted_iota(jnp.int32, (SIDE, SIDE), 0)
     column = lax.broadcasted_iota(jnp.int32, (SIDE, SIDE), 1)
     mean_diag = jnp.where(row == column, float(PART), 0.0)
@@ -88,10 +92,7 @@
             if i == j:
                 block = block - mean_diag
             packed_ref[place(i, j) : place(i, j) + SIDE] = block.astype(jnp.bfloat16)
-
-
-def mine_kernel(raw_ref, other_ref, mine_ref, terms_ref):
-    mine_ref[...], scaling = normalize(raw_ref[...])
+    mine_ref[...], scaling = normalize(whole_ref[:, :, core].reshape(BATCH, PART))
     both = mine_ref[...].astype(jnp.float32) * other_ref[...].astype(jnp.float32)
     on_diag = jnp.sum(both, axis=0, keepdims=True) / BATCH
     terms_ref[0:1] = scaling
@@ -135,8 +136,10 @@
     squares, first, second = squares / (BATCH * BATCH), first / BATCH, second / BATCH
     loss = (1.0 - on_diag) * (1.0 - on_diag) + LAMBDA * (squares - on_diag * on_diag)
     for k in range(SLICES):
+        places = [CHIPS.index(h * SLICES + k) for h in range(GROUPS)]
+        order = sum(jnp.where(group == h, places[h], 0) for h in range(GROUPS))
         for c in range(2):
-            start = ((group * SLICES + k) * 2 + c) * ROWS
+            start = c * (BATCH // 2) + order * ROWS
             rows = pl.ds(pl.multiple_of(start, ROWS), ROWS)
             held = mine_ref[rows].astype(jnp.float32)
             grad = scaling * (up_ref[rows] - first - held * second)
@@ -172,30 +175,35 @@
 def local(view_one, view_two):
     bf16, f32 = jnp.bfloat16, jnp.float32
     shape = jax.ShapeDtypeStruct
-    group = lax.axis_index("zh").astype(jnp.int32).reshape(1)
+    device = lax.axis_index("batch").astype(jnp.int32).reshape(1)
+    core, group = device % 2, device // 8
 
     sent = pl.pallas_call(
         spread_kernel,
-        out_shape=pltpu.VMEM((2 * OWNERS, ROWS, PART), bf16),
+        out_shape=pltpu.VMEM((OWNERS, 2, ROWS, PART), bf16),
         in_specs=[pl.BlockSpec(memory_space=pl.ANY)] * 2,
         out_specs=pl.BlockSpec(memory_space=pltpu.VMEM),
         scratch_shapes=[pltpu.VMEM((2, ROWS, WIDTH), bf16), pltpu.SemaphoreType.DMA((2,))],
     )(view_one, view_two)
-    raw = swap(sent, IMAGES).reshape(BATCH, PART)
-    raw_mine = lax.ppermute(raw, "c", [(0, 1), (1, 0)])
-
-    other, packed = call(
+    sent, core, group = lax.optimization_barrier((sent, core, group))
+    whole = lax.all_gather(swap(sent, "batch", SAME_CORE), "batch", axis_index_groups=CORES)
+
+    mine, other, terms, packed = call(
         gram_kernel,
-        [shape((BATCH, PART), bf16), shape((PACKED, SIDE), bf16)],
+        [
+            pltpu.VMEM((BATCH, PART), bf16),
+            pltpu.VMEM((BATCH, PART), bf16),
+            pltpu.VMEM((8, PART), f32),
+            pltpu.VMEM((PACKED, SIDE), bf16),
+        ],
         2 * BATCH * BATCH * PART,
-        raw,
-    )
-    mine, terms = call(
-        mine_kernel, [shape((BATCH, PART), bf16), shape((8, PART), f32)], 0, raw_mine, other
-    )
-    strips = swap(packed.reshape(OWNERS, CHUNK, SIDE), FEAT)
-    strips = swap(call(sum_kernel, shape((SLICES, CHUNK, SIDE), bf16), 0, strips), "zl")
-    strips = swap(call(sum_kernel, shape((OWNERS, CHUNK, SIDE), bf16), 0, strips), FEAT)
+        core,
+        whole,
+        scalars=1,
+    )
+    strips = swap(packed.reshape(OWNERS, CHUNK, SIDE), "feat")
+    strips = swap(call(sum_kernel, shape((SLICES, CHUNK, SIDE), bf16), 0, strips), "batch", NEAR)
+    strips = swap(call(sum_kernel, shape((OWNERS, CHUNK, SIDE), bf16), 0, strips), "feat")
 
     out = call(
         apply_kernel,
@@ -213,14 +221,13 @@
         unpack_kernel,
         [shape((1, WIDTH), f32), shape((ROWS, WIDTH), f32), shape((ROWS, WIDTH), f32)],
         0,
-        swap(out, ("zl", "c")),
+        swap(out, "batch", GROUP),
     )
     return (loss.reshape(WIDTH), one, two)
 
 
 def solution(mesh):
-    cut = Mesh(mesh.devices.reshape(CUTS), NAMES)
-    spread = P(IMAGES, FEAT)
+    spread = P("batch", "feat")
     return jax.shard_map(
-        local, mesh=cut, in_specs=(spread, spread), out_specs=(P(FEAT), spread, spread), check_vma=False
-    )
+        local, mesh=mesh, in_specs=(spread, spread), out_specs=(P("feat"), spread, spread), check_vma=False
+    )

time: 88.4 us -> 85.5 us (0.967)
  blocking collectives: 72.6 us -> 81.9 us
  starting transfers between devices: 8 us -> 0 us
  waiting for transfers between devices: 3.17 us -> 0 us
  Pallas kernels: 3.51 us -> 2.61 us
    all_gather x0 -> x1, blocking collectives: none -> 8.57 us  [local(): lax.all_gather(swap(sent, 'batch', SAME_CORE), 'batch', axis_index_groups...]
    ppermute x1 -> x0, starting transfers between devices: 4.46 us -> none  [local(): raw_mine = lax.ppermute(raw, 'c', [(0, 1), (1, 0)])]
    all_to_all x1 -> x0, starting transfers between devices: 3.54 us -> none  [swap(): return lax.all_to_all(values, axes, split_axis=0, concat_axis=0)]
    all_to_all x1 -> x0, waiting for transfers between devices: 2.04 us -> none  [swap(): return lax.all_to_all(values, axes, split_axis=0, concat_axis=0)]
    ppermute x1 -> x0, waiting for transfers between devices: 1.14 us -> none  [local(): raw_mine = lax.ppermute(raw, 'c', [(0, 1), (1, 0)])]
    pallas_call x6 -> x5, Pallas kernels: 2.7 us -> 1.8 us  [call(): pl.pallas_call(kernel, out_shape=out_shape, in_specs=specs, out_specs=[wh...]
    all_to_all x4 -> x5, blocking collectives: 72.6 us -> 73.3 us  [swap(): lax.all_to_all(values, axis, split_axis=0, concat_axis=0, axis_index_grou...]
  transfers between devices with their start and end apart: 2 -> 0, of which waited for: 2 -> 0; matrix products, arithmetic and copies ran while one was open for 0% -> 0% of each run, Pallas kernels for 0% -> 0%
where the time goes in v5:
time: 85.5 us; the launch traced here: 85.2 us
  blocking collectives  81.9 us (96%)
  Pallas kernels  2.61 us (3%)
    all_to_all x5, blocking collectives, swap(): lax.all_to_all(values, axis, split_axis=0, concat_axis=0, axis_index_grou...  73.3 us
    all_gather x1, blocking collectives, local(): lax.all_gather(swap(sent, 'batch', SAME_CORE), 'batch', axis_index_groups...  8.57 us
    pallas_call x5, Pallas kernels, call(): pl.pallas_call(kernel, out_shape=out_shape, in_specs=specs, out_specs=[wh...  1.8 us

profile of v5, /device:TPU:1, one launch (start us, length us, event | category | flops | bytes accessed | tf_op | source)
XLA Modules:
  0.0 85.2 jit_solution(5111500914775804186)
XLA Ops:
  0.7 0.8 shard_map.49
  1.5 28.5 %all_to_all.25 = bf16[16,2,16,256]{3,2,1,0:T(8,128)(2,1)S(1)} all-to-all(bf16[16,2,16,256]{3,2,1,0:T(8,128)(2,1)S(1)} %shard_map.49), channel_id=1, replica_groups={{0,128,64,192,32,160,96,224,256,384,320,448,288,416,352,480},{16,144,80..., dimensions={0} | all-to-all | bytes 524288 | tf_op jit(solution)/shard_map/all_to_all | solution.py:35
  30.0 8.6 %all-gather = bf16[32,2,16,256]{3,2,1,0:T(8,128)(2,1)S(1)} all-gather(bf16[16,2,16,256]{3,2,1,0:T(8,128)(2,1)S(1)} %all_to_all.25), channel_id=2, replica_groups={{0,16},{32,48},{64,80},{96,112},{128,144},{160,176},{192,208},{224,240}..., dimensions={0}, use_global_device_ids=true | all-gather | bytes 786432 | tf_op jit(solution)/shard_map/all_gather | solution.py:189
  38.5 0.5 shard_map.50
  39.1 15.4 %all_to_all.26.parts_ref = bf16[16,80,128]{2,1,0:T(8,128)(2,1)S(1)} all-to-all(bf16[16,80,128]{2,1,0:T(8,128)(2,1)S(1)} %bitcast.7), channel_id=1, replica_groups=mesh['batch'=32,'feat'=16] {'feat'}, dimensions={0} | all-to-all | bytes 655360 | tf_op jit(solution)/shard_map/all_to_all | solution.py:35
  54.5 7.0 %all_to_all.27.parts_ref = bf16[4,80,128]{2,1,0:T(8,128)(2,1)S(1)} all-to-all(bf16[4,80,128]{2,1,0:T(8,128)(2,1)S(1)} %shard_map.51), channel_id=1, replica_groups={{0,64,32,96},{16,80,48,112},{128,192,160,224},{144,208,176,240},{256,32..., dimensions={0} | all-to-all | bytes 163840 | tf_op jit(solution)/shard_map/all_to_all | solution.py:35
  61.5 10.8 %all_to_all.28 = bf16[16,80,128]{2,1,0:T(8,128)(2,1)S(1)} all-to-all(bf16[16,80,128]{2,1,0:T(8,128)(2,1)S(1)} %shard_map.52), channel_id=1, replica_groups=mesh['batch'=32,'feat'=16] {'feat'}, dimensions={0} | all-to-all | bytes 655360 | tf_op jit(solution)/shard_map/all_to_all | solution.py:35
  72.3 0.5 shard_map.53
  72.9 11.6 %all_to_all.29.parts_ref = bf16[8,16,384]{2,1,0:T(8,128)(2,1)S(1)} all-to-all(bf16[8,16,384]{2,1,0:T(8,128)(2,1)S(1)} %shard_map.53), channel_id=1, replica_groups={{0,16,32,48,64,80,96,112},{128,144,160,176,192,208,224,240},{256,272,28..., dimensions={0} | all-to-all | bytes 196608 | tf_op jit(solution)/shard_map/all_to_all | solution.py:35
  84.5 0.7 shard_map.54
  (2 shorter events, 0.1 us)

commit v6 on v5

--- a/solution.py
+++ b/solution.py
@@ -10,7 +10,10 @@
 FEATURES = 16384
 BATCH = 512
 
-CHIPS = (0, 4, 2, 6, 1, 5, 3, 7, 8, 12, 10, 14, 9, 13, 11, 15)
+CHIPS = (8, 7, 9, 6, 10, 5, 11, 4, 12, 3, 13, 2, 14, 1, 15, 0)
+NEAR = (1, 2, 0, 3)
+OWNER = (2, 3, 4, 5, 0, 1, 6, 7)
+FEAT = (5, 6, 9, 10, 4, 7, 1, 2, 8, 11, 13, 14, 0, 3, 12, 15)
 GROUPS = 4
 SLICES = 4
 OWNERS = 16
@@ -27,8 +30,8 @@
 
 SAME_CORE = [[2 * z + c for z in CHIPS] for c in range(2)]
 CORES = [[2 * z, 2 * z + 1] for z in range(16)]
-NEAR = [[8 * h + 2 * k + c for k in (0, 2, 1, 3)] for h in range(4) for c in range(2)]
-GROUP = [list(range(8 * h, 8 * h + 8)) for h in range(4)]
+NEIGHBOURS = [[8 * h + 2 * k + c for k in NEAR] for h in range(4) for c in range(2)]
+GROUP = [[8 * h + i for i in OWNER] for h in range(4)]
 
 
 def swap(values, axis, groups=None):
@@ -143,7 +146,7 @@
             rows = pl.ds(pl.multiple_of(start, ROWS), ROWS)
             held = mine_ref[rows].astype(jnp.float32)
             grad = scaling * (up_ref[rows] - first - held * second)
-            out_ref[2 * k + c, :, :PART] = grad.astype(jnp.bfloat16)
+            out_ref[OWNER.index(2 * k + c), :, :PART] = grad.astype(jnp.bfloat16)
     high = loss.astype(jnp.bfloat16)
     rest = loss - high.astype(jnp.float32)
     middle = rest.astype(jnp.bfloat16)
@@ -163,9 +166,9 @@
     halves = PART // SIDE
     for k in range(SLICES):
         columns = slice(k * PART, (k + 1) * PART)
-        one_ref[:, columns] = parts_ref[2 * k, :, :PART].astype(jnp.float32)
-        two_ref[:, columns] = parts_ref[2 * k + 1, :, :PART].astype(jnp.float32)
-        tail = parts_ref[2 * k, :, PART:].astype(jnp.float32)
+        one_ref[:, columns] = parts_ref[OWNER.index(2 * k), :, :PART].astype(jnp.float32)
+        two_ref[:, columns] = parts_ref[OWNER.index(2 * k + 1), :, :PART].astype(jnp.float32)
+        tail = parts_ref[OWNER.index(2 * k), :, PART:].astype(jnp.float32)
         for half in range(halves):
             high, middle, low = [tail[n * halves + half : n * halves + half + 1] for n in range(3)]
             start = k * PART + half * SIDE
@@ -201,9 +204,9 @@
         whole,
         scalars=1,
     )
-    strips = swap(packed.reshape(OWNERS, CHUNK, SIDE), "feat")
-    strips = swap(call(sum_kernel, shape((SLICES, CHUNK, SIDE), bf16), 0, strips), "batch", NEAR)
-    strips = swap(call(sum_kernel, shape((OWNERS, CHUNK, SIDE), bf16), 0, strips), "feat")
+    strips = swap(packed.reshape(OWNERS, CHUNK, SIDE), "feat", [list(FEAT)])
+    strips = swap(call(sum_kernel, shape((SLICES, CHUNK, SIDE), bf16), 0, strips), "batch", NEIGHBOURS)
+    strips = swap(call(sum_kernel, shape((OWNERS, CHUNK, SIDE), bf16), 0, strips), "feat", [list(FEAT)])
 
     out = call(
         apply_kernel,

time: 85.5 us -> 81.5 us (0.953)
  blocking collectives: 81.9 us -> 77.9 us
    all_gather x1, blocking collectives: 8.57 us -> 3.44 us  [local(): lax.all_gather(swap(sent, 'batch', SAME_CORE), 'batch', axis_index_groups...]
    all_to_all x5, blocking collectives: 73.3 us -> 74.5 us  [swap(): lax.all_to_all(values, axis, split_axis=0, concat_axis=0, axis_index_grou...]
where the time goes in v6:
time: 81.5 us; the launch traced here: 81.2 us
  blocking collectives  77.9 us (96%)
  Pallas kernels  2.6 us (3%)
    all_to_all x5, blocking collectives, swap(): lax.all_to_all(values, axis, split_axis=0, concat_axis=0, axis_index_grou...  74.5 us
    all_gather x1, blocking collectives, local(): lax.all_gather(swap(sent, 'batch', SAME_CORE), 'batch', axis_index_groups...  3.44 us
    pallas_call x5, Pallas kernels, call(): pl.pallas_call(kernel, out_shape=out_shape, in_specs=specs, out_specs=[wh...  1.8 us

profile of v6, /device:TPU:1, one launch (start us, length us, event | category | flops | bytes accessed | tf_op | source)
XLA Modules:
  0.0 81.2 jit_solution(3521563807809434383)
XLA Ops:
  0.7 0.8 shard_map.49
  1.5 30.5 %all_to_all.25 = bf16[16,2,16,256]{3,2,1,0:T(8,128)(2,1)S(1)} all-to-all(bf16[16,2,16,256]{3,2,1,0:T(8,128)(2,1)S(1)} %shard_map.49), channel_id=1, replica_groups={{256,224,288,192,320,160,352,128,384,96,416,64,448,32,480,0},{272,240,3..., dimensions={0} | all-to-all | bytes 524288 | tf_op jit(solution)/shard_map/all_to_all | solution.py:38
  32.0 3.4 %all-gather = bf16[32,2,16,256]{3,2,1,0:T(8,128)(2,1)S(1)} all-gather(bf16[16,2,16,256]{3,2,1,0:T(8,128)(2,1)S(1)} %all_to_all.25), channel_id=2, replica_groups={{0,16},{32,48},{64,80},{96,112},{128,144},{160,176},{192,208},{224,240}..., dimensions={0}, use_global_device_ids=true | all-gather | bytes 786432 | tf_op jit(solution)/shard_map/all_gather | solution.py:192
  35.5 0.5 shard_map.50
  36.0 15.3 %all_to_all.26.parts_ref = bf16[16,80,128]{2,1,0:T(8,128)(2,1)S(1)} all-to-all(bf16[16,80,128]{2,1,0:T(8,128)(2,1)S(1)} %bitcast.7), channel_id=1, replica_groups={{5,6,9,10,4,7,1,2,8,11,13,14,0,3,12,15},{21,22,25,26,20,23,17,18,24,27,..., dimensions={0} | all-to-all | bytes 655360 | tf_op jit(solution)/shard_map/all_to_all | solution.py:38
  51.3 7.3 %all_to_all.27.parts_ref = bf16[4,80,128]{2,1,0:T(8,128)(2,1)S(1)} all-to-all(bf16[4,80,128]{2,1,0:T(8,128)(2,1)S(1)} %shard_map.51), channel_id=1, replica_groups={{32,64,0,96},{48,80,16,112},{160,192,128,224},{176,208,144,240},{288,32..., dimensions={0} | all-to-all | bytes 163840 | tf_op jit(solution)/shard_map/all_to_all | solution.py:38
  58.7 10.8 %all_to_all.28 = bf16[16,80,128]{2,1,0:T(8,128)(2,1)S(1)} all-to-all(bf16[16,80,128]{2,1,0:T(8,128)(2,1)S(1)} %shard_map.52), channel_id=1, replica_groups={{5,6,9,10,4,7,1,2,8,11,13,14,0,3,12,15},{21,22,25,26,20,23,17,18,24,27,..., dimensions={0} | all-to-all | bytes 655360 | tf_op jit(solution)/shard_map/all_to_all | solution.py:38
  69.5 0.5 shard_map.53
  70.0 10.5 %all_to_all.29.parts_ref = bf16[8,16,384]{2,1,0:T(8,128)(2,1)S(1)} all-to-all(bf16[8,16,384]{2,1,0:T(8,128)(2,1)S(1)} %shard_map.53), channel_id=1, replica_groups={{32,48,64,80,0,16,96,112},{160,176,192,208,128,144,224,240},{288,304,32..., dimensions={0} | all-to-all | bytes 196608 | tf_op jit(solution)/shard_map/all_to_all | solution.py:38
  80.5 0.7 shard_map.54
  (2 shorter events, 0.1 us)

commit v7 on v6

--- a/solution.py
+++ b/solution.py
@@ -10,10 +10,10 @@
 FEATURES = 16384
 BATCH = 512
 
-CHIPS = (8, 7, 9, 6, 10, 5, 11, 4, 12, 3, 13, 2, 14, 1, 15, 0)
+CHIPS = (10, 9, 11, 8, 12, 7, 13, 6, 14, 5, 15, 4, 3, 2, 1, 0)
 NEAR = (1, 2, 0, 3)
 OWNER = (2, 3, 4, 5, 0, 1, 6, 7)
-FEAT = (5, 6, 9, 10, 4, 7, 1, 2, 8, 11, 13, 14, 0, 3, 12, 15)
+FEAT = (10, 11, 12, 13, 14, 15, 0, 1, 2, 3, 4, 5, 6, 7, 8, 9)
 GROUPS = 4
 SLICES = 4
 OWNERS = 16

time: 81.5 us -> 77.3 us (0.948)
  blocking collectives: 77.9 us -> 73.7 us
    all_to_all x5, blocking collectives: 74.5 us -> 69.3 us  [swap(): lax.all_to_all(values, axis, split_axis=0, concat_axis=0, axis_index_grou...]
    all_gather x1, blocking collectives: 3.44 us -> 4.4 us  [local(): lax.all_gather(swap(sent, 'batch', SAME_CORE), 'batch', axis_index_groups...]
where the time goes in v7:
time: 77.3 us; the launch traced here: 77 us
  blocking collectives  73.7 us (95%)
  Pallas kernels  2.6 us (3%)
    all_to_all x5, blocking collectives, swap(): lax.all_to_all(values, axis, split_axis=0, concat_axis=0, axis_index_grou...  69.3 us
    all_gather x1, blocking collectives, local(): lax.all_gather(swap(sent, 'batch', SAME_CORE), 'batch', axis_index_groups...  4.4 us
    pallas_call x5, Pallas kernels, call(): pl.pallas_call(kernel, out_shape=out_shape, in_specs=specs, out_specs=[wh...  1.8 us

profile of v7, /device:TPU:1, one launch (start us, length us, event | category | flops | bytes accessed | tf_op | source)
XLA Modules:
  0.0 77.0 jit_solution(16441702288485481349)
XLA Ops:
  0.7 0.8 %shard_map.49 = bf16[16,2,16,256]{3,2,1,0:T(8,128)(2,1)S(1)} custom-call(bf16[16,1024]{1,0:T(8,128)(2,1)} %one_ref.1, bf16[16,1024]{1,0:T(8,128)(2,1)} %two_ref.1), custom_call_target="tpu_custom_call" | custom-call | tf_op jit(solution)/shard_map/pallas_call | solution.py:184
  1.5 29.5 %all_to_all.25 = bf16[16,2,16,256]{3,2,1,0:T(8,128)(2,1)S(1)} all-to-all(bf16[16,2,16,256]{3,2,1,0:T(8,128)(2,1)S(1)} %shard_map.49), channel_id=1, replica_groups={{320,288,352,256,384,224,416,192,448,160,480,128,96,64,32,0},{336,304,3..., dimensions={0} | all-to-all | bytes 524288 | tf_op jit(solution)/shard_map/all_to_all | solution.py:38
  31.0 4.4 %all-gather = bf16[32,2,16,256]{3,2,1,0:T(8,128)(2,1)S(1)} all-gather(bf16[16,2,16,256]{3,2,1,0:T(8,128)(2,1)S(1)} %all_to_all.25), channel_id=2, replica_groups={{0,16},{32,48},{64,80},{96,112},{128,144},{160,176},{192,208},{224,240}..., dimensions={0}, use_global_device_ids=true | all-gather | bytes 786432 | tf_op jit(solution)/shard_map/all_gather | solution.py:192
  35.4 0.5 shard_map.50
  35.9 12.7 %all_to_all.26.parts_ref = bf16[16,80,128]{2,1,0:T(8,128)(2,1)S(1)} all-to-all(bf16[16,80,128]{2,1,0:T(8,128)(2,1)S(1)} %bitcast.7), channel_id=1, replica_groups={{10,11,12,13,14,15,0,1,2,3,4,5,6,7,8,9},{26,27,28,29,30,31,16,17,18,19,..., dimensions={0} | all-to-all | bytes 655360 | tf_op jit(solution)/shard_map/all_to_all | solution.py:38
  48.7 6.5 %all_to_all.27.parts_ref = bf16[4,80,128]{2,1,0:T(8,128)(2,1)S(1)} all-to-all(bf16[4,80,128]{2,1,0:T(8,128)(2,1)S(1)} %shard_map.51), channel_id=1, replica_groups={{32,64,0,96},{48,80,16,112},{160,192,128,224},{176,208,144,240},{288,32..., dimensions={0} | all-to-all | bytes 163840 | tf_op jit(solution)/shard_map/all_to_all | solution.py:38
  55.2 10.1 %all_to_all.28 = bf16[16,80,128]{2,1,0:T(8,128)(2,1)S(1)} all-to-all(bf16[16,80,128]{2,1,0:T(8,128)(2,1)S(1)} %shard_map.52), channel_id=1, replica_groups={{10,11,12,13,14,15,0,1,2,3,4,5,6,7,8,9},{26,27,28,29,30,31,16,17,18,19,..., dimensions={0} | all-to-all | bytes 655360 | tf_op jit(solution)/shard_map/all_to_all | solution.py:38
  65.3 0.5 shard_map.53
  65.9 10.5 %all_to_all.29.parts_ref = bf16[8,16,384]{2,1,0:T(8,128)(2,1)S(1)} all-to-all(bf16[8,16,384]{2,1,0:T(8,128)(2,1)S(1)} %shard_map.53), channel_id=1, replica_groups={{32,48,64,80,0,16,96,112},{160,176,192,208,128,144,224,240},{288,304,32..., dimensions={0} | all-to-all | bytes 196608 | tf_op jit(solution)/shard_map/all_to_all | solution.py:38
  76.3 0.7 shard_map.54
  (2 shorter events, 0.1 us)

commit v8 on v7

--- a/solution.py
+++ b/solution.py
@@ -10,7 +10,7 @@
 FEATURES = 16384
 BATCH = 512
 
-CHIPS = (10, 9, 11, 8, 12, 7, 13, 6, 14, 5, 15, 4, 3, 2, 1, 0)
+CHIPS = (11, 12, 13, 14, 15, 0, 1, 2, 3, 4, 5, 6, 7, 8, 9, 10)
 NEAR = (1, 2, 0, 3)
 OWNER = (2, 3, 4, 5, 0, 1, 6, 7)
 FEAT = (10, 11, 12, 13, 14, 15, 0, 1, 2, 3, 4, 5, 6, 7, 8, 9)

time: 77.3 us -> 77.2 us (level)
    all_gather x1, blocking collectives: 4.4 us -> 3.12 us  [local(): lax.all_gather(swap(sent, 'batch', SAME_CORE), 'batch', axis_index_groups...]
    all_to_all x5, blocking collectives: 69.3 us -> 70.4 us  [swap(): lax.all_to_all(values, axis, split_axis=0, concat_axis=0, axis_index_grou...]
where the time goes in v8:
time: 77.2 us; the launch traced here: 76.8 us
  blocking collectives  73.5 us (95%)
  Pallas kernels  2.6 us (3%)
    all_to_all x5, blocking collectives, swap(): lax.all_to_all(values, axis, split_axis=0, concat_axis=0, axis_index_grou...  70.4 us
    all_gather x1, blocking collectives, local(): lax.all_gather(swap(sent, 'batch', SAME_CORE), 'batch', axis_index_groups...  3.12 us
    pallas_call x5, Pallas kernels, call(): pl.pallas_call(kernel, out_shape=out_shape, in_specs=specs, out_specs=[wh...  1.8 us

profile of v8, /device:TPU:1, one launch (start us, length us, event | category | flops | bytes accessed | tf_op | source)
XLA Modules:
  0.0 76.8 jit_solution(7832598967608345142)
XLA Ops:
  0.7 0.8 %shard_map.49 = bf16[16,2,16,256]{3,2,1,0:T(8,128)(2,1)S(1)} custom-call(bf16[16,1024]{1,0:T(8,128)(2,1)} %one_ref.1, bf16[16,1024]{1,0:T(8,128)(2,1)} %two_ref.1), custom_call_target="tpu_custom_call" | custom-call | tf_op jit(solution)/shard_map/pallas_call | solution.py:184
  1.5 30.8 %all_to_all.25 = bf16[16,2,16,256]{3,2,1,0:T(8,128)(2,1)S(1)} all-to-all(bf16[16,2,16,256]{3,2,1,0:T(8,128)(2,1)S(1)} %shard_map.49), channel_id=1, replica_groups={{352,384,416,448,480,0,32,64,96,128,160,192,224,256,288,320},{368,400,4..., dimensions={0} | all-to-all | bytes 524288 | tf_op jit(solution)/shard_map/all_to_all | solution.py:38
  32.2 3.1 %all-gather = bf16[32,2,16,256]{3,2,1,0:T(8,128)(2,1)S(1)} all-gather(bf16[16,2,16,256]{3,2,1,0:T(8,128)(2,1)S(1)} %all_to_all.25), channel_id=2, replica_groups={{0,16},{32,48},{64,80},{96,112},{128,144},{160,176},{192,208},{224,240}..., dimensions={0}, use_global_device_ids=true | all-gather | bytes 786432 | tf_op jit(solution)/shard_map/all_gather | solution.py:192
  35.4 0.5 shard_map.50
  35.9 12.8 %all_to_all.26.parts_ref = bf16[16,80,128]{2,1,0:T(8,128)(2,1)S(1)} all-to-all(bf16[16,80,128]{2,1,0:T(8,128)(2,1)S(1)} %bitcast.7), channel_id=1, replica_groups={{10,11,12,13,14,15,0,1,2,3,4,5,6,7,8,9},{26,27,28,29,30,31,16,17,18,19,..., dimensions={0} | all-to-all | bytes 655360 | tf_op jit(solution)/shard_map/all_to_all | solution.py:38
  48.7 6.2 %all_to_all.27.parts_ref = bf16[4,80,128]{2,1,0:T(8,128)(2,1)S(1)} all-to-all(bf16[4,80,128]{2,1,0:T(8,128)(2,1)S(1)} %shard_map.51), channel_id=1, replica_groups={{32,64,0,96},{48,80,16,112},{160,192,128,224},{176,208,144,240},{288,32..., dimensions={0} | all-to-all | bytes 163840 | tf_op jit(solution)/shard_map/all_to_all | solution.py:38
  54.9 10.1 %all_to_all.28 = bf16[16,80,128]{2,1,0:T(8,128)(2,1)S(1)} all-to-all(bf16[16,80,128]{2,1,0:T(8,128)(2,1)S(1)} %shard_map.52), channel_id=1, replica_groups={{10,11,12,13,14,15,0,1,2,3,4,5,6,7,8,9},{26,27,28,29,30,31,16,17,18,19,..., dimensions={0} | all-to-all | bytes 655360 | tf_op jit(solution)/shard_map/all_to_all | solution.py:38
  65.0 0.5 shard_map.53
  65.6 10.6 %all_to_all.29.parts_ref = bf16[8,16,384]{2,1,0:T(8,128)(2,1)S(1)} all-to-all(bf16[8,16,384]{2,1,0:T(8,128)(2,1)S(1)} %shard_map.53), channel_id=1, replica_groups={{32,48,64,80,0,16,96,112},{160,176,192,208,128,144,224,240},{288,304,32..., dimensions={0} | all-to-all | bytes 196608 | tf_op jit(solution)/shard_map/all_to_all | solution.py:38
  76.2 0.7 shard_map.54
  (2 shorter events, 0.1 us)

commit v9 on v8

--- a/solution.py
+++ b/solution.py
@@ -10,7 +10,7 @@
 FEATURES = 16384
 BATCH = 512
 
-CHIPS = (11, 12, 13, 14, 15, 0, 1, 2, 3, 4, 5, 6, 7, 8, 9, 10)
+CHIPS = (12, 13, 14, 15, 0, 1, 2, 3, 4, 5, 6, 7, 8, 9, 10, 11)
 NEAR = (1, 2, 0, 3)
 OWNER = (2, 3, 4, 5, 0, 1, 6, 7)
 FEAT = (10, 11, 12, 13, 14, 15, 0, 1, 2, 3, 4, 5, 6, 7, 8, 9)

time: 77.2 us -> 78.5 us (1.017)
  blocking collectives: 73.5 us -> 74.9 us
    all_gather x1, blocking collectives: 3.12 us -> 6.23 us  [local(): lax.all_gather(swap(sent, 'batch', SAME_CORE), 'batch', axis_index_groups...]
    all_to_all x5, blocking collectives: 70.4 us -> 68.6 us  [swap(): lax.all_to_all(values, axis, split_axis=0, concat_axis=0, axis_index_grou...]
where the time goes in v9:
time: 78.5 us; the launch traced here: 78.1 us
  blocking collectives  74.9 us (95%)
  Pallas kernels  2.6 us (3%)
    all_to_all x5, blocking collectives, swap(): lax.all_to_all(values, axis, split_axis=0, concat_axis=0, axis_index_grou...  68.6 us
    all_gather x1, blocking collectives, local(): lax.all_gather(swap(sent, 'batch', SAME_CORE), 'batch', axis_index_groups...  6.23 us
    pallas_call x5, Pallas kernels, call(): pl.pallas_call(kernel, out_shape=out_shape, in_specs=specs, out_specs=[wh...  1.8 us

profile of v9, /device:TPU:1, one launch (start us, length us, event | category | flops | bytes accessed | tf_op | source)
XLA Modules:
  0.0 78.1 jit_solution(9560039674591346409)
XLA Ops:
  0.7 0.8 %shard_map.49 = bf16[16,2,16,256]{3,2,1,0:T(8,128)(2,1)S(1)} custom-call(bf16[16,1024]{1,0:T(8,128)(2,1)} %one_ref.1, bf16[16,1024]{1,0:T(8,128)(2,1)} %two_ref.1), custom_call_target="tpu_custom_call" | custom-call | tf_op jit(solution)/shard_map/pallas_call | solution.py:184
  1.5 29.0 %all_to_all.25 = bf16[16,2,16,256]{3,2,1,0:T(8,128)(2,1)S(1)} all-to-all(bf16[16,2,16,256]{3,2,1,0:T(8,128)(2,1)S(1)} %shard_map.49), channel_id=1, replica_groups={{384,416,448,480,0,32,64,96,128,160,192,224,256,288,320,352},{400,432,4..., dimensions={0} | all-to-all | bytes 524288 | tf_op jit(solution)/shard_map/all_to_all | solution.py:38
  30.5 6.2 %all-gather = bf16[32,2,16,256]{3,2,1,0:T(8,128)(2,1)S(1)} all-gather(bf16[16,2,16,256]{3,2,1,0:T(8,128)(2,1)S(1)} %all_to_all.25), channel_id=2, replica_groups={{0,16},{32,48},{64,80},{96,112},{128,144},{160,176},{192,208},{224,240}..., dimensions={0}, use_global_device_ids=true | all-gather | bytes 786432 | tf_op jit(solution)/shard_map/all_gather | solution.py:192
  36.7 0.5 shard_map.50
  37.2 12.7 %all_to_all.26.parts_ref = bf16[16,80,128]{2,1,0:T(8,128)(2,1)S(1)} all-to-all(bf16[16,80,128]{2,1,0:T(8,128)(2,1)S(1)} %bitcast.7), channel_id=1, replica_groups={{10,11,12,13,14,15,0,1,2,3,4,5,6,7,8,9},{26,27,28,29,30,31,16,17,18,19,..., dimensions={0} | all-to-all | bytes 655360 | tf_op jit(solution)/shard_map/all_to_all | solution.py:38
  50.0 6.5 %all_to_all.27.parts_ref = bf16[4,80,128]{2,1,0:T(8,128)(2,1)S(1)} all-to-all(bf16[4,80,128]{2,1,0:T(8,128)(2,1)S(1)} %shard_map.51), channel_id=1, replica_groups={{32,64,0,96},{48,80,16,112},{160,192,128,224},{176,208,144,240},{288,32..., dimensions={0} | all-to-all | bytes 163840 | tf_op jit(solution)/shard_map/all_to_all | solution.py:38
  56.5 10.1 %all_to_all.28 = bf16[16,80,128]{2,1,0:T(8,128)(2,1)S(1)} all-to-all(bf16[16,80,128]{2,1,0:T(8,128)(2,1)S(1)} %shard_map.52), channel_id=1, replica_groups={{10,11,12,13,14,15,0,1,2,3,4,5,6,7,8,9},{26,27,28,29,30,31,16,17,18,19,..., dimensions={0} | all-to-all | bytes 655360 | tf_op jit(solution)/shard_map/all_to_all | solution.py:38
  66.6 0.5 shard_map.53
  67.1 10.3 %all_to_all.29.parts_ref = bf16[8,16,384]{2,1,0:T(8,128)(2,1)S(1)} all-to-all(bf16[8,16,384]{2,1,0:T(8,128)(2,1)S(1)} %shard_map.53), channel_id=1, replica_groups={{32,48,64,80,0,16,96,112},{160,176,192,208,128,144,224,240},{288,304,32..., dimensions={0} | all-to-all | bytes 196608 | tf_op jit(solution)/shard_map/all_to_all | solution.py:38
  77.5 0.7 shard_map.54
  (2 shorter events, 0.1 us)

commit v10 on v8

--- a/solution.py
+++ b/solution.py
@@ -13,7 +13,7 @@
 CHIPS = (11, 12, 13, 14, 15, 0, 1, 2, 3, 4, 5, 6, 7, 8, 9, 10)
 NEAR = (1, 2, 0, 3)
 OWNER = (2, 3, 4, 5, 0, 1, 6, 7)
-FEAT = (10, 11, 12, 13, 14, 15, 0, 1, 2, 3, 4, 5, 6, 7, 8, 9)
+FEAT = (10, 11, 14, 15, 9, 8, 13, 12, 6, 7, 2, 3, 5, 4, 1, 0)
 GROUPS = 4
 SLICES = 4
 OWNERS = 16

time: 77.2 us -> 77.2 us (level)
  no operation moved by 1% of the time
where the time goes in v10:
time: 77.2 us; the launch traced here: 76.8 us
  blocking collectives  73.6 us (95%)
  Pallas kernels  2.6 us (3%)
    all_to_all x5, blocking collectives, swap(): lax.all_to_all(values, axis, split_axis=0, concat_axis=0, axis_index_grou...  70.4 us
    all_gather x1, blocking collectives, local(): lax.all_gather(swap(sent, 'batch', SAME_CORE), 'batch', axis_index_groups...  3.12 us
    pallas_call x5, Pallas kernels, call(): pl.pallas_call(kernel, out_shape=out_shape, in_specs=specs, out_specs=[wh...  1.8 us

profile of v10, /device:TPU:1, one launch (start us, length us, event | category | flops | bytes accessed | tf_op | source)
XLA Modules:
  0.0 76.8 jit_solution(16878349567423415674)
XLA Ops:
  0.7 0.8 %shard_map.49 = bf16[16,2,16,256]{3,2,1,0:T(8,128)(2,1)S(1)} custom-call(bf16[16,1024]{1,0:T(8,128)(2,1)} %one_ref.1, bf16[16,1024]{1,0:T(8,128)(2,1)} %two_ref.1), custom_call_target="tpu_custom_call" | custom-call | tf_op jit(solution)/shard_map/pallas_call | solution.py:184
  1.5 30.8 %all_to_all.25 = bf16[16,2,16,256]{3,2,1,0:T(8,128)(2,1)S(1)} all-to-all(bf16[16,2,16,256]{3,2,1,0:T(8,128)(2,1)S(1)} %shard_map.49), channel_id=1, replica_groups={{352,384,416,448,480,0,32,64,96,128,160,192,224,256,288,320},{368,400,4..., dimensions={0} | all-to-all | bytes 524288 | tf_op jit(solution)/shard_map/all_to_all | solution.py:38
  32.2 3.1 %all-gather = bf16[32,2,16,256]{3,2,1,0:T(8,128)(2,1)S(1)} all-gather(bf16[16,2,16,256]{3,2,1,0:T(8,128)(2,1)S(1)} %all_to_all.25), channel_id=2, replica_groups={{0,16},{32,48},{64,80},{96,112},{128,144},{160,176},{192,208},{224,240}..., dimensions={0}, use_global_device_ids=true | all-gather | bytes 786432 | tf_op jit(solution)/shard_map/all_gather | solution.py:192
  35.4 0.5 shard_map.50
  35.9 12.2 %all_to_all.26.parts_ref = bf16[16,80,128]{2,1,0:T(8,128)(2,1)S(1)} all-to-all(bf16[16,80,128]{2,1,0:T(8,128)(2,1)S(1)} %bitcast.7), channel_id=1, replica_groups={{10,11,14,15,9,8,13,12,6,7,2,3,5,4,1,0},{26,27,30,31,25,24,29,28,22,23,..., dimensions={0} | all-to-all | bytes 655360 | tf_op jit(solution)/shard_map/all_to_all | solution.py:38
  48.2 6.3 %all_to_all.27.parts_ref = bf16[4,80,128]{2,1,0:T(8,128)(2,1)S(1)} all-to-all(bf16[4,80,128]{2,1,0:T(8,128)(2,1)S(1)} %shard_map.51), channel_id=1, replica_groups={{32,64,0,96},{48,80,16,112},{160,192,128,224},{176,208,144,240},{288,32..., dimensions={0} | all-to-all | bytes 163840 | tf_op jit(solution)/shard_map/all_to_all | solution.py:38
  54.5 9.9 %all_to_all.28 = bf16[16,80,128]{2,1,0:T(8,128)(2,1)S(1)} all-to-all(bf16[16,80,128]{2,1,0:T(8,128)(2,1)S(1)} %shard_map.52), channel_id=1, replica_groups={{10,11,14,15,9,8,13,12,6,7,2,3,5,4,1,0},{26,27,30,31,25,24,29,28,22,23,..., dimensions={0} | all-to-all | bytes 655360 | tf_op jit(solution)/shard_map/all_to_all | solution.py:38
  64.4 0.5 shard_map.53
  64.9 11.3 %all_to_all.29.parts_ref = bf16[8,16,384]{2,1,0:T(8,128)(2,1)S(1)} all-to-all(bf16[8,16,384]{2,1,0:T(8,128)(2,1)S(1)} %shard_map.53), channel_id=1, replica_groups={{32,48,64,80,0,16,96,112},{160,176,192,208,128,144,224,240},{288,304,32..., dimensions={0} | all-to-all | bytes 196608 | tf_op jit(solution)/shard_map/all_to_all | solution.py:38
  76.2 0.7 shard_map.54
  (2 shorter events, 0.1 us)
